TPU v7x, 32 devices: a whole 2x2x4 slice. The times are simulated.
32 devices in a mesh: section: 1, expert: 32 (over z, y, x, core).
Axes of the slice: x: 2, y: 2, z: 4, core: 2. Of those that a mesh axis runs over, the one named last changes fastest.
Arguments:
- states_orig: bfloat16 [1, 256, 2048], P(None, 'expert'), may hold values from -400 to 400
- states_pruned: bfloat16 [1, 256, 2048], P(None, 'expert'), may hold values from -400 to 400
- ids_orig: int32 [1, 1, 256, 8], P('section', None, 'expert'), may hold values from 0 to 15, all different within a row; in each aligned block of 8 rows (0 to 7, 8 to 15, ..., all dimensions but the last counted through in order) at most 8 rows name the same one
- ids_pruned: int32 [1, 1, 256, 8], P('section', None, 'expert'), may hold values from 0 to 15, all different within a row; in each aligned block of 8 rows (0 to 7, 8 to 15, ..., all dimensions but the last counted through in order) at most 8 rows name the same one
- gates_orig: float32 [1, 1, 256, 8], P('section', None, 'expert'), may hold values from 0.02 to 2.7
- gates_pruned: float32 [1, 1, 256, 8], P('section', None, 'expert'), may hold values from 0.02 to 2.7
- keep_mask: int32 [1, 16], P('section'), may hold values 0 or 1
- w_in: bfloat16 [1, 32, 2048, 768], P('section', 'expert'), may hold values from -0.125 to 0.125
- w_out: bfloat16 [1, 32, 384, 2048], P('section', 'expert'), may hold values from -0.21875 to 0.21875
Outputs:
- moe_orig: bfloat16 [1, 1, 256, 2048], P('section', None, 'expert')
- moe_pruned: bfloat16 [1, 1, 256, 2048], P('section', None, 'expert')
- expert_loss: float32 [1, 16], P('section')
Inputs may be any that keep to these rules, and one draw needn't show every extreme that they name: `ids_orig`: for each layer, micro-batch and device along expert, no expert is picked by more than 8 of that device's 8 tokens, and some expert is picked by exactly 8. The 8 picks of a token are different experts. `ids_pruned`: for each layer, micro-batch and device along expert, no expert is picked by more than 8 of that device's 8 tokens, and some expert is picked by exactly 8. The 8 picks of a token are different experts. `keep_mask`: 1 keeps an expert in the pruned model, 0 removes it.
All inputs are finite; a program needn't handle non-finite values. No bound on the sum of `keep_mask` on one device may be relied on, other than what follows from the above.
Results may differ from a plain program's by a relative error of at most 0.012.
Values may be sent and summed in bfloat16 or wider, within the bound.
No kernel may reach another device: no remote copies, remote signals or barrier semaphores. Data moves between devices by JAX's collectives and lax.ppermute only.
A program may use at most 64 MiB of HBM per device.

v0:
```python
import functools

import jax
import jax.numpy as jnp
from jax import lax
from jax.experimental import pallas as pl
from jax.experimental.pallas import tpu as pltpu
from jax.sharding import PartitionSpec as P

SPLIT = 2
LANES = 128
MIB = 2**20


def run_kernel(body, outs, operands, scratch=(), limit=16, space=pltpu.VMEM):
    return pl.pallas_call(
        body,
        out_shape=outs,
        in_specs=[pl.BlockSpec(memory_space=space)] * len(operands),
        out_specs=jax.tree.map(lambda _: pl.BlockSpec(memory_space=pltpu.VMEM), outs),
        scratch_shapes=list(scratch),
        compiler_params=pltpu.CompilerParams(vmem_limit_bytes=limit * MIB),
    )(*operands)


def in_hbm(value):
    return pltpu.with_memory_space_constraint(value, pltpu.HBM)


def like(rows, columns, dtype=jnp.bfloat16):
    return jax.ShapeDtypeStruct((rows, columns), dtype)


def exclusive(value, mask):
    pairs = [(source, source ^ mask) for source in range(lax.axis_size("expert"))]
    return lax.ppermute(value, "expert", pairs)


def normalize_rows(values):
    factor = lax.rsqrt(jnp.mean(values * values, axis=-1, keepdims=True) + 1e-06)
    return values * factor


def dense_weights(picked, gates, experts):
    rows = picked.shape[0]
    label = lax.broadcasted_iota(jnp.int32, (rows, experts), 1)
    total = jnp.zeros((rows, experts), jnp.float32)
    for k in range(picked.shape[1]):
        total = total + jnp.where(picked[:, k : k + 1] == label, gates[:, k : k + 1], 0.0)
    return total


def pack_kernel(count, *refs):
    sources, out_ref, scratch = refs[:count], refs[count], refs[count + 1 :]
    held, sems = scratch[:count], scratch[count]
    copies = [
        pltpu.make_async_copy(source, target, sems.at[place])
        for place, (source, target) in enumerate(zip(sources, held))
    ]
    for copy in copies:
        copy.start()
    for copy in copies:
        copy.wait()
    so_ref, sp_ref, io_ref, ip_ref, go_ref, gp_ref, keep_ref = held
    model_width = so_ref.shape[1]
    extra = out_ref.shape[1] - model_width
    experts = keep_ref.shape[1]
    states = jnp.concatenate(
        [so_ref[...].astype(jnp.float32), sp_ref[...].astype(jnp.float32)], axis=0
    )
    out_ref[:, :model_width] = normalize_rows(states).astype(jnp.bfloat16)
    dense_orig = dense_weights(io_ref[...], go_ref[...], experts)
    dense_pruned = dense_weights(ip_ref[...], gp_ref[...], experts)
    dense_pruned = dense_pruned * keep_ref[...].astype(jnp.float32)
    dense = jnp.concatenate([dense_orig, dense_pruned], axis=0)
    high = dense.astype(jnp.bfloat16)
    low = (dense - high.astype(jnp.float32)).astype(jnp.bfloat16)
    source = lax.broadcasted_iota(jnp.int32, (experts, extra), 0)
    lane = lax.broadcasted_iota(jnp.int32, (experts, extra), 1)
    out_ref[:, model_width:] = (
        jnp.dot(
            high,
            (lane == source).astype(jnp.float32).astype(jnp.bfloat16),
            preferred_element_type=jnp.float32,
        )
        + jnp.dot(
            low,
            (lane == source + experts).astype(jnp.float32).astype(jnp.bfloat16),
            preferred_element_type=jnp.float32,
        )
    ).astype(jnp.bfloat16)


def stage_kernel(count, *refs):
    sources, targets, sems = refs[:count], refs[count : 2 * count], refs[2 * count]
    copies = [
        pltpu.make_async_copy(source, target, sems.at[place])
        for place, (source, target) in enumerate(zip(sources, targets))
    ]
    for copy in copies:
        copy.start()
    for copy in copies:
        copy.wait()


def stage(arrays):
    return run_kernel(
        functools.partial(stage_kernel, len(arrays)),
        [pltpu.VMEM(value.shape, value.dtype) for value in arrays],
        arrays,
        [pltpu.SemaphoreType.DMA((len(arrays),))],
        space=pl.ANY,
    )


def after(value, *awaited):
    return lax.optimization_barrier((value, awaited))[0]


def join_kernel(*refs):
    part_refs, out_ref = refs[:-1], refs[-1]
    rows = part_refs[0].shape[0]
    for place, part_ref in enumerate(part_refs):
        out_ref[place * rows : (place + 1) * rows, :] = part_ref[...]


def join_rows(parts):
    rows, columns = parts[0].shape
    return run_kernel(join_kernel, like(len(parts) * rows, columns), parts)


def expert_kernel(experts, row_count, sizes, *refs):
    row_refs, refs = refs[:row_count], refs[row_count:]
    in_refs, out_refs, refs = refs[:SPLIT], refs[SPLIT : 2 * SPLIT], refs[2 * SPLIT :]
    result_refs, (rows, hidden) = refs[: len(sizes)], refs[len(sizes) :]
    half, model_width = out_refs[0].shape
    expert = lax.axis_index("expert") // SPLIT
    weights = []
    filled = 0
    for row_ref in row_refs:
        size = row_ref.shape[0]
        rows[filled : filled + size, :] = row_ref[:, :model_width]
        filled += size
        extra = row_ref[:, model_width:].astype(jnp.float32)
        lane = lax.broadcasted_iota(jnp.int32, extra.shape, 1)
        mine = jnp.logical_or(lane == expert, lane == expert + experts)
        weights.append(jnp.sum(jnp.where(mine, extra, 0.0), axis=1, keepdims=True))
    weight = jnp.concatenate(weights, axis=0)
    for place, in_ref in enumerate(in_refs):
        both = jnp.dot(rows[...], in_ref[...], preferred_element_type=jnp.float32)
        gate, up = both[:, :half], both[:, half:]
        hidden[:, place * half : (place + 1) * half] = (
            gate / (1.0 + jnp.exp(-gate)) * up
        ).astype(jnp.bfloat16)
    step = min(512, model_width)
    for start in range(0, model_width, step):
        value = sum(
            jnp.dot(
                hidden[:, place * half : (place + 1) * half],
                out_ref[:, start : start + step],
                preferred_element_type=jnp.float32,
            )
            for place, out_ref in enumerate(out_refs)
        )
        value = (value * weight).astype(jnp.bfloat16)
        filled = 0
        for size, result_ref in zip(sizes, result_refs):
            result_ref[:, start : start + step] = value[filled : filled + size]
            filled += size


def run_expert(experts, row_arrays, weights, sizes):
    total = sum(array.shape[0] for array in row_arrays)
    half, model_width = weights[-1].shape
    return run_kernel(
        functools.partial(expert_kernel, experts, len(row_arrays), sizes),
        [like(size, model_width) for size in sizes],
        list(row_arrays) + list(weights),
        [
            pltpu.VMEM((total, model_width), jnp.bfloat16),
            pltpu.VMEM((total, SPLIT * half), jnp.bfloat16),
        ],
        limit=24,
    )


def plane_kernel(count, *refs):
    part_refs, out_refs = refs[:count], refs[count:]
    rows = out_refs[0].shape[0]
    for place, out_ref in enumerate(out_refs):
        out_ref[...] = sum(
            ref[place * rows : (place + 1) * rows, :].astype(jnp.float32) for ref in part_refs
        ).astype(out_ref.dtype)


def final_kernel(parts, factor, *refs):
    part_refs, refs = refs[:parts], refs[parts:]
    ids_ref, gates_ref, orig_ref, pruned_ref, terms_ref, *value_refs = refs
    tok_rows = orig_ref.shape[0]
    total = sum(ref[...].astype(jnp.float32) for ref in part_refs)
    for value_ref in value_refs:
        value_ref[...] = total
    value_orig, value_pruned = total[:tok_rows], total[tok_rows:]
    orig_ref[...] = value_orig.astype(jnp.bfloat16)
    pruned_ref[...] = value_pruned.astype(jnp.bfloat16)
    differ = value_orig - value_pruned
    errors = jnp.mean(differ * differ, axis=1, keepdims=True)
    experts = terms_ref.shape[1]
    dense = dense_weights(ids_ref[...], gates_ref[...], experts)
    terms = factor * jnp.sum(dense * errors, axis=0, keepdims=True)
    terms_ref[...] = jnp.broadcast_to(terms, terms_ref.shape)


def add_kernel(parts_ref, out_ref):
    out_ref[...] = jnp.sum(parts_ref[...], axis=0, keepdims=True)


def on_device(
    states_orig,
    states_pruned,
    ids_orig,
    ids_pruned,
    gates_orig,
    gates_pruned,
    keep_mask,
    w_in,
    w_out,
):
    devices = lax.axis_size("expert")
    section_count = lax.axis_size("section")
    section_index = lax.axis_index("section")
    micro_count, tok_rows, model_width = states_orig.shape
    experts = keep_mask.shape[1]
    top_count = ids_orig.shape[-1]
    loss_factor = experts / (top_count * micro_count * tok_rows * devices)
    extra = -(-2 * experts // LANES) * LANES
    rows = 2 * tok_rows
    chips = devices // SPLIT
    inner = min(4, chips)
    outer = chips // inner
    inner_masks = [SPLIT * i for i in range(1, inner)]
    layer_mask = lambda j: SPLIT * inner * j
    nearer = list(range(1, outer // 2 + 1))
    streams = [[j for j in range(outer) if j not in nearer], nearer]
    own_in, own_out = w_in[0, 0], w_out[0, 0]
    other_out, other_in = exclusive(own_out, 1), exclusive(own_in, 1)

    step_count = micro_count + section_count - 1
    carry = jnp.zeros((2, tok_rows, model_width), jnp.bfloat16)
    moe_orig = jnp.zeros((micro_count, tok_rows, model_width), jnp.bfloat16)
    moe_pruned = moe_orig
    terms = jnp.zeros((devices, experts), jnp.float32)
    for tick in range(step_count):
        if section_count == 1:
            position = tick
            item = lambda buffer: buffer[position]
        else:
            position = jnp.clip(tick - section_index, 0, micro_count - 1)
            active = jnp.logical_and(
                tick - section_index >= 0, tick - section_index < micro_count
            )
            item = lambda buffer: lax.dynamic_index_in_dim(buffer, position, 0, keepdims=False)
        fresh = min(tick, micro_count - 1)
        state_orig, state_pruned = states_orig[fresh], states_pruned[fresh]
        if section_count > 1:
            state_orig = jnp.where(section_index == 0, state_orig, carry[0])
            state_pruned = jnp.where(section_index == 0, state_pruned, carry[1])
        picked_orig, weight_orig = item(ids_orig[0]), item(gates_orig[0])
        operands = [
            state_orig,
            state_pruned,
            picked_orig,
            item(ids_pruned[0]),
            weight_orig,
            item(gates_pruned[0]),
            keep_mask,
        ]
        packed = run_kernel(
            functools.partial(pack_kernel, len(operands)),
            like(rows, model_width + extra),
            [in_hbm(value) for value in operands],
            [pltpu.VMEM(value.shape, value.dtype) for value in operands]
            + [pltpu.SemaphoreType.DMA((len(operands),))],
            space=pl.ANY,
        )
        column = {0: packed}
        for j in streams[1][::-1] + streams[0][1:]:
            column[j] = exclusive(packed, layer_mask(j))
        if tick == 0:
            own = stage([in_hbm(own_in), in_hbm(own_out)])
            weights = [own[0], other_in, own[1], other_out]
        blocks = []
        for stream, layers in enumerate(streams):
            joined = join_rows([column[j] for j in layers])
            if stream == 1:
                joined = after(joined, own, other_in, other_out)
            block = [joined]
            for mask in inner_masks:
                block.append(exclusive(joined, mask))
            blocks.append(block)
        summed = []
        for stream, layers in enumerate(streams):
            partial = run_expert(
                experts, blocks[stream], weights, [len(layers) * rows] * inner
            )
            returned = [partial[0]] + [
                exclusive(part, mask) for part, mask in zip(partial[1:], inner_masks)
            ]
            outs = [like(rows, model_width)] * len(layers)
            if stream == 0:
                outs[0] = like(rows, model_width, jnp.float32)
            sums = run_kernel(functools.partial(plane_kernel, inner), outs, returned)
            for j, value in list(zip(layers, sums))[::-1]:
                summed.append(exclusive(value, layer_mask(j)) if j else value)
        round_orig, round_pruned, tick_terms, *moe = run_kernel(
            functools.partial(final_kernel, outer, loss_factor),
            [like(tok_rows, model_width)] * 2
            + [like(devices, experts, jnp.float32)]
            + [like(rows, model_width, jnp.float32)] * (section_count > 1),
            summed + [picked_orig, weight_orig],
        )
        if section_count > 1:
            tick_terms = jnp.where(active, tick_terms, 0.0)
            round_orig = jnp.where(active, round_orig, item(moe_orig))
            round_pruned = jnp.where(active, round_pruned, item(moe_pruned))
        terms = tick_terms if tick == 0 else terms + tick_terms
        moe_orig = lax.dynamic_update_index_in_dim(moe_orig, round_orig, position, 0)
        moe_pruned = lax.dynamic_update_index_in_dim(moe_pruned, round_pruned, position, 0)
        if tick + 1 < step_count and section_count > 1:
            state = jnp.stack([state_orig, state_pruned]).astype(jnp.float32)
            following = (state + moe[0].reshape(state.shape)).astype(jnp.bfloat16)
            onward = [(i, i + 1) for i in range(section_count - 1)]
            carry = lax.ppermute(following, "section", onward)
    shared = lax.all_to_all(terms, "expert", split_axis=0, concat_axis=0, tiled=True)
    loss = run_kernel(add_kernel, like(1, experts, jnp.float32), [shared])
    return (moe_orig[None], moe_pruned[None], loss)


def solution(mesh):
    return jax.shard_map(
        on_device,
        mesh=mesh,
        in_specs=(
            P(None, "expert", None),
            P(None, "expert", None),
            P("section", None, "expert", None),
            P("section", None, "expert", None),
            P("section", None, "expert", None),
            P("section", None, "expert", None),
            P("section", None),
            P("section", "expert", None, None),
            P("section", "expert", None, None),
        ),
        out_specs=(
            P("section", None, "expert", None),
            P("section", None, "expert", None),
            P("section", None),
        ),
        check_vma=False,
    )
```

profile of v0, /device:TPU:0, one launch (start us, length us, event | category | flops | bytes accessed | tf_op | source)
XLA Modules:
  0.0 56.3 jit_solution(1878493139767299980)
XLA Ops:
  0.6 0.5 collective-permute-start.4
  1.1 0.1 collective-permute-start.5
  1.2 1.1 %shard_map.112.refs_0_ = bf16[16,2176]{1,0:T(8,128)(2,1)S(1)} custom-call(bf16[8,2048]{1,0:T(8,128)(2,1)} %bitcast.24, bf16[8,2048]{1,0:T(8,128)(2,1)} %bitcast.25, s32[8,8]{1,0:T(8,128)} %bitcast.15, s32[8,8]{1,0:T(8,128)} %bitcast.26, f32[8,8]{1,0:T(8,128)} %bitcast.17, f32[8,8]{1,0:T(8,128)} %bitcast.27, s32[1,16]{1,0:T(1,128)} %refs_6_.1), custom_call_target="tpu_custom_call" | custom-call | tf_op jit(solution)/shard_map/pallas_call | solution.py:16
  2.3 5.1 %collective-permute-start = (bf16[16,2176]{1,0:T(8,128)(2,1)S(1)}, bf16[16,2176]{1,0:T(8,128)(2,1)S(1)}, u32[]{:S(2)}, u32[]{:S(2)}) collective-permute-start(bf16[16,2176]{1,0:T(8,128)(2,1)S(1)} %shard_map.112.refs_0_), channel_id=1, source_target_pairs={{0,24},{1,25},{2,26},{3,27},{4,28},{5,29},{6,30},{7,31},{8,16},{9,... | collective-permute-start | bytes 208904 | tf_op jit(solution)/shard_map/ppermute | solution.py:36
  7.4 0.0 collective-permute-start.10
  7.4 0.6 %collective-permute-start.11 = (bf16[16,2176]{1,0:T(8,128)(2,1)S(1)}, bf16[16,2176]{1,0:T(8,128)(2,1)S(1)}, u32[]{:S(2)}, u32[]{:S(2)}) collective-permute-start(bf16[16,2176]{1,0:T(8,128)(2,1)S(1)} %shard_map.112.refs_0_), channel_id=1, source_target_pairs={{0,16},{1,17},{2,18},{3,19},{4,20},{5,21},{6,22},{7,23},{8,24},{9,... | collective-permute-start | bytes 208904 | tf_op jit(solution)/shard_map/ppermute | solution.py:36
  8.1 2.3 %collective-permute-done.refs_1_ = bf16[16,2176]{1,0:T(8,128)(2,1)S(1)} collective-permute-done((bf16[16,2176]{1,0:T(8,128)(2,1)S(1)}, bf16[16,2176]{1,0:T(8,128)(2,1)S(1)}, u32[]{:S(2)}, u32[]{:S(2)}) %collective-permute-start) | collective-permute-done | bytes 69664 | tf_op jit(solution)/shard_map/ppermute | solution.py:36
  10.4 1.8 %collective-permute-start.1 = (bf16[32,2176]{1,0:T(8,128)(2,1)S(1)}, bf16[32,2176]{1,0:T(8,128)(2,1)S(1)}, u32[]{:S(2)}, u32[]{:S(2)}) collective-permute-start(bf16[32,2176]{1,0:T(8,128)(2,1)S(1)} %shard_map.113.refs_0_), channel_id=1, source_target_pairs={{0,2},{1,3},{2,0},{3,1},{4,6},{5,7},{6,4},{7,5},{8,10},{9,11},{10,... | collective-permute-start | bytes 417800 | tf_op jit(solution)/shard_map/ppermute | solution.py:36
  12.3 0.2 collective-permute-done.10.refs_0_
  12.4 1.6 %collective-permute-start.2 = (bf16[32,2176]{1,0:T(8,128)(2,1)S(1)}, bf16[32,2176]{1,0:T(8,128)(2,1)S(1)}, u32[]{:S(2)}, u32[]{:S(2)}) collective-permute-start(bf16[32,2176]{1,0:T(8,128)(2,1)S(1)} %shard_map.113.refs_0_), channel_id=1, source_target_pairs={{0,4},{1,5},{2,6},{3,7},{4,0},{5,1},{6,2},{7,3},{8,12},{9,13},{10,... | collective-permute-start | bytes 417800 | tf_op jit(solution)/shard_map/ppermute | solution.py:36
  14.1 0.0 collective-permute-done.11.refs_1_
  14.1 1.7 %collective-permute-start.3 = (bf16[32,2176]{1,0:T(8,128)(2,1)S(1)}, bf16[32,2176]{1,0:T(8,128)(2,1)S(1)}, u32[]{:S(2)}, u32[]{:S(2)}) collective-permute-start(bf16[32,2176]{1,0:T(8,128)(2,1)S(1)} %shard_map.113.refs_0_), channel_id=1, source_target_pairs={{0,6},{1,7},{2,4},{3,5},{4,2},{5,3},{6,0},{7,1},{8,14},{9,15},{10,... | collective-permute-start | bytes 417800 | tf_op jit(solution)/shard_map/ppermute | solution.py:36
  15.8 2.4 %shard_map.114 = (bf16[2048,768]{1,0:T(8,128)(2,1)S(1)}, bf16[384,2048]{1,0:T(8,128)(2,1)S(1)}) custom-call(bf16[2048,768]{1,0:T(8,128)(2,1)} %bitcast.21, bf16[384,2048]{1,0:T(8,128)(2,1)} %bitcast.23), custom_call_target="tpu_custom_call" | custom-call | tf_op jit(solution)/shard_map/pallas_call | solution.py:16
  18.2 0.0 collective-permute-done.5.refs_7_
  18.2 0.0 collective-permute-done.4.refs_5_
  18.2 0.6 %collective-permute-start.12 = (bf16[32,2176]{1,0:T(8,128)(2,1)S(1)}, bf16[32,2176]{1,0:T(8,128)(2,1)S(1)}, u32[]{:S(2)}, u32[]{:S(2)}) collective-permute-start(bf16[32,2176]{1,0:T(8,128)(2,1)S(1)} %shard_map.117.refs_0_), channel_id=1, source_target_pairs={{0,2},{1,3},{2,0},{3,1},{4,6},{5,7},{6,4},{7,5},{8,10},{9,11},{10,... | collective-permute-start | bytes 417800 | tf_op jit(solution)/shard_map/ppermute | solution.py:36
  18.8 1.2 %collective-permute-start.13 = (bf16[32,2176]{1,0:T(8,128)(2,1)S(1)}, bf16[32,2176]{1,0:T(8,128)(2,1)S(1)}, u32[]{:S(2)}, u32[]{:S(2)}) collective-permute-start(bf16[32,2176]{1,0:T(8,128)(2,1)S(1)} %shard_map.117.refs_0_), channel_id=1, source_target_pairs={{0,4},{1,5},{2,6},{3,7},{4,0},{5,1},{6,2},{7,3},{8,12},{9,13},{10,... | collective-permute-start | bytes 417800 | tf_op jit(solution)/shard_map/ppermute | solution.py:36
  20.1 0.0 collective-permute-done.1.refs_1_
  20.1 1.7 %collective-permute-start.14 = (bf16[32,2176]{1,0:T(8,128)(2,1)S(1)}, bf16[32,2176]{1,0:T(8,128)(2,1)S(1)}, u32[]{:S(2)}, u32[]{:S(2)}) collective-permute-start(bf16[32,2176]{1,0:T(8,128)(2,1)S(1)} %shard_map.117.refs_0_), channel_id=1, source_target_pairs={{0,6},{1,7},{2,4},{3,5},{4,2},{5,3},{6,0},{7,1},{8,14},{9,15},{10,... | collective-permute-start | bytes 417800 | tf_op jit(solution)/shard_map/ppermute | solution.py:36
  21.8 0.0 collective-permute-done.2.refs_2_
  21.8 0.0 collective-permute-done.3.refs_3_
  21.8 1.7 %shard_map.115 = (bf16[32,2048]{1,0:T(8,128)(2,1)S(1)}, bf16[32,2048]{1,0:T(8,128)(2,1)S(1)}, bf16[32,2048]{1,0:T(8,128)(2,1)S(1)}, bf16[32,2048]{1,0:T(8,128)(2,1)S(1)}) custom-call(bf16[32,2176]{1,0:T(8,128)(2,1)S(1)} %shard_map.113.refs_0_, bf16[32,2176]{1,0:T(8,128)(2,1)S(1)} %collective-permute-done.1.refs_1_, ...), custom_call_target="tpu_custom_call" | custom-call | tf_op jit(solution)/shard_map/pallas_call | solution.py:16
  23.5 0.9 %collective-permute-start.6 = (bf16[32,2048]{1,0:T(8,128)(2,1)S(1)}, bf16[32,2048]{1,0:T(8,128)(2,1)S(1)}, u32[]{:S(2)}, u32[]{:S(2)}) collective-permute-start(bf16[32,2048]{1,0:T(8,128)(2,1)S(1)} %get-tuple-element.24), channel_id=1, source_target_pairs={{0,2},{1,3},{2,0},{3,1},{4,6},{5,7},{6,4},{7,5},{8,10},{9,11},{10,... | collective-permute-start | bytes 393224 | tf_op jit(solution)/shard_map/ppermute | solution.py:36
  24.5 1.8 %collective-permute-start.7 = (bf16[32,2048]{1,0:T(8,128)(2,1)S(1)}, bf16[32,2048]{1,0:T(8,128)(2,1)S(1)}, u32[]{:S(2)}, u32[]{:S(2)}) collective-permute-start(bf16[32,2048]{1,0:T(8,128)(2,1)S(1)} %get-tuple-element.25), channel_id=1, source_target_pairs={{0,4},{1,5},{2,6},{3,7},{4,0},{5,1},{6,2},{7,3},{8,12},{9,13},{10,... | collective-permute-start | bytes 393224 | tf_op jit(solution)/shard_map/ppermute | solution.py:36
  26.3 0.0 collective-permute-done.12.refs_1_
  26.3 1.3 %collective-permute-start.8 = (bf16[32,2048]{1,0:T(8,128)(2,1)S(1)}, bf16[32,2048]{1,0:T(8,128)(2,1)S(1)}, u32[]{:S(2)}, u32[]{:S(2)}) collective-permute-start(bf16[32,2048]{1,0:T(8,128)(2,1)S(1)} %get-tuple-element.26), channel_id=1, source_target_pairs={{0,6},{1,7},{2,4},{3,5},{4,2},{5,3},{6,0},{7,1},{8,14},{9,15},{10,... | collective-permute-start | bytes 393224 | tf_op jit(solution)/shard_map/ppermute | solution.py:36
  27.6 0.0 collective-permute-done.13.refs_2_
  27.6 0.4 collective-permute-done.14.refs_3_
  27.9 1.6 %shard_map.118 = (bf16[32,2048]{1,0:T(8,128)(2,1)S(1)}, bf16[32,2048]{1,0:T(8,128)(2,1)S(1)}, bf16[32,2048]{1,0:T(8,128)(2,1)S(1)}, bf16[32,2048]{1,0:T(8,128)(2,1)S(1)}) custom-call(bf16[32,2176]{1,0:T(8,128)(2,1)S(1)} %shard_map.117.refs_0_, bf16[32,2176]{1,0:T(8,128)(2,1)S(1)} %collective-permute-done.12.refs_1_, ...), custom_call_target="tpu_custom_call" | custom-call | tf_op jit(solution)/shard_map/pallas_call | solution.py:16
  29.6 1.2 %collective-permute-start.15 = (bf16[32,2048]{1,0:T(8,128)(2,1)S(1)}, bf16[32,2048]{1,0:T(8,128)(2,1)S(1)}, u32[]{:S(2)}, u32[]{:S(2)}) collective-permute-start(bf16[32,2048]{1,0:T(8,128)(2,1)S(1)} %get-tuple-element.31), channel_id=1, source_target_pairs={{0,2},{1,3},{2,0},{3,1},{4,6},{5,7},{6,4},{7,5},{8,10},{9,11},{10,... | collective-permute-start | bytes 393224 | tf_op jit(solution)/shard_map/ppermute | solution.py:36
  30.8 2.5 %collective-permute-start.16 = (bf16[32,2048]{1,0:T(8,128)(2,1)S(1)}, bf16[32,2048]{1,0:T(8,128)(2,1)S(1)}, u32[]{:S(2)}, u32[]{:S(2)}) collective-permute-start(bf16[32,2048]{1,0:T(8,128)(2,1)S(1)} %get-tuple-element.32), channel_id=1, source_target_pairs={{0,4},{1,5},{2,6},{3,7},{4,0},{5,1},{6,2},{7,3},{8,12},{9,13},{10,... | collective-permute-start | bytes 393224 | tf_op jit(solution)/shard_map/ppermute | solution.py:36
  33.3 0.0 collective-permute-done.6.refs_1_
  33.3 0.0 collective-permute-start.17
  33.3 0.0 collective-permute-done.7.refs_2_
  33.3 0.8 %collective-permute-done.8.refs_3_ = bf16[32,2048]{1,0:T(8,128)(2,1)S(1)} collective-permute-done((bf16[32,2048]{1,0:T(8,128)(2,1)S(1)}, bf16[32,2048]{1,0:T(8,128)(2,1)S(1)}, u32[]{:S(2)}, u32[]{:S(2)}) %collective-permute-start.8) | collective-permute-done | bytes 131104 | tf_op jit(solution)/shard_map/ppermute | solution.py:36
  34.1 0.1 shard_map.116
  34.2 3.1 %collective-permute-start.9 = (bf16[16,2048]{1,0:T(8,128)(2,1)S(1)}, bf16[16,2048]{1,0:T(8,128)(2,1)S(1)}, u32[]{:S(2)}, u32[]{:S(2)}) collective-permute-start(bf16[16,2048]{1,0:T(8,128)(2,1)S(1)} %get-tuple-element.27), channel_id=1, source_target_pairs={{0,24},{1,25},{2,26},{3,27},{4,28},{5,29},{6,30},{7,31},{8,16},{9,... | collective-permute-start | bytes 196616 | tf_op jit(solution)/shard_map/ppermute | solution.py:36
  37.2 0.0 collective-permute-done.15.refs_1_
  37.2 0.0 collective-permute-done.16.refs_2_
  37.2 1.9 %collective-permute-done.17.refs_3_ = bf16[32,2048]{1,0:T(8,128)(2,1)S(1)} collective-permute-done((bf16[32,2048]{1,0:T(8,128)(2,1)S(1)}, bf16[32,2048]{1,0:T(8,128)(2,1)S(1)}, u32[]{:S(2)}, u32[]{:S(2)}) %collective-permute-start.17) | collective-permute-done | bytes 131104 | tf_op jit(solution)/shard_map/ppermute | solution.py:36
  39.2 0.1 shard_map.119
  39.2 0.5 collective-permute-start.18
  39.7 1.9 %collective-permute-start.19 = (bf16[16,2048]{1,0:T(8,128)(2,1)S(1)}, bf16[16,2048]{1,0:T(8,128)(2,1)S(1)}, u32[]{:S(2)}, u32[]{:S(2)}) collective-permute-start(bf16[16,2048]{1,0:T(8,128)(2,1)S(1)} %get-tuple-element.35), channel_id=1, source_target_pairs={{0,8},{1,9},{2,10},{3,11},{4,12},{5,13},{6,14},{7,15},{8,0},{9,1},... | collective-permute-start | bytes 196616 | tf_op jit(solution)/shard_map/ppermute | solution.py:36
  41.6 3.1 %collective-permute-done.18.refs_2_ = bf16[16,2048]{1,0:T(8,128)(2,1)S(1)} collective-permute-done((bf16[16,2048]{1,0:T(8,128)(2,1)S(1)}, bf16[16,2048]{1,0:T(8,128)(2,1)S(1)}, u32[]{:S(2)}, u32[]{:S(2)}) %collective-permute-start.18) | collective-permute-done | bytes 65568 | tf_op jit(solution)/shard_map/ppermute | solution.py:36
  44.7 0.0 collective-permute-done.19.refs_3_
  44.7 0.7 %shard_map.120 = (bf16[8,2048]{1,0:T(8,128)(2,1)}, bf16[8,2048]{1,0:T(8,128)(2,1)}, f32[32,16]{1,0:T(8,128)S(1)}) custom-call(bf16[16,2048]{1,0:T(8,128)(2,1)S(1)} %collective-permute-done.9.refs_0_, f32[16,2048]{1,0:T(8,128)S(1)} %get-tuple-element.28.refs_1_, bf16[16,2048]{1,0:T(8,128)(2,1)S(1)} %collective-permute-done.18.refs_2_, ...), custom_call_target="tpu_custom_call" | custom-call | tf_op jit(solution)/shard_map/pallas_call | solution.py:16
  45.4 10.3 %all_to_all.11 = f32[32,1,16]{2,1,0:T(1,128)S(1)} all-to-all(f32[32,1,16]{2,1,0:T(1,128)S(1)} %bitcast.19), channel_id=1, replica_groups=mesh['section'=1,'expert'=32] {'expert'}, dimensions={0} | all-to-all | bytes 4096 | tf_op jit(solution)/shard_map/all_to_all | solution.py:334
  55.8 0.5 shard_map.121
  (7 shorter events, 0.0 us)
Async XLA Ops:
  0.6 17.6 %collective-permute-start.4 = (bf16[2048,768]{1,0:T(8,128)(2,1)}, bf16[2048,768]{1,0:T(8,128)(2,1)S(1)}, u32[]{:S(2)}, u32[]{:S(2)}) collective-permute-start(bf16[2048,768]{1,0:T(8,128)(2,1)} %bitcast.20), channel_id=1, source_target_pairs={{0,1},{1,0},{2,3},{3,2},{4,5},{5,4},{6,7},{7,6},{8,9},{9,8},{10,11... | collective-permute-start | bytes 9437192 | tf_op jit(solution)/shard_map/ppermute | solution.py:36
  1.1 17.1 %collective-permute-start.5 = (bf16[384,2048]{1,0:T(8,128)(2,1)}, bf16[384,2048]{1,0:T(8,128)(2,1)S(1)}, u32[]{:S(2)}, u32[]{:S(2)}) collective-permute-start(bf16[384,2048]{1,0:T(8,128)(2,1)} %bitcast.22), channel_id=1, source_target_pairs={{0,1},{1,0},{2,3},{3,2},{4,5},{5,4},{6,7},{7,6},{8,9},{9,8},{10,11... | collective-permute-start | bytes 4718600 | tf_op jit(solution)/shard_map/ppermute | solution.py:36
  2.3 8.1 %collective-permute-start = (bf16[16,2176]{1,0:T(8,128)(2,1)S(1)}, bf16[16,2176]{1,0:T(8,128)(2,1)S(1)}, u32[]{:S(2)}, u32[]{:S(2)}) collective-permute-start(bf16[16,2176]{1,0:T(8,128)(2,1)S(1)} %shard_map.112.refs_0_), channel_id=1, source_target_pairs={{0,24},{1,25},{2,26},{3,27},{4,28},{5,29},{6,30},{7,31},{8,16},{9,... | collective-permute-start | bytes 208904 | tf_op jit(solution)/shard_map/ppermute | solution.py:36
  7.4 5.0 %collective-permute-start.10 = (bf16[16,2176]{1,0:T(8,128)(2,1)S(1)}, bf16[16,2176]{1,0:T(8,128)(2,1)S(1)}, u32[]{:S(2)}, u32[]{:S(2)}) collective-permute-start(bf16[16,2176]{1,0:T(8,128)(2,1)S(1)} %shard_map.112.refs_0_), channel_id=1, source_target_pairs={{0,8},{1,9},{2,10},{3,11},{4,12},{5,13},{6,14},{7,15},{8,0},{9,1},... | collective-permute-start | bytes 208904 | tf_op jit(solution)/shard_map/ppermute | solution.py:36
  7.4 6.7 %collective-permute-start.11 = (bf16[16,2176]{1,0:T(8,128)(2,1)S(1)}, bf16[16,2176]{1,0:T(8,128)(2,1)S(1)}, u32[]{:S(2)}, u32[]{:S(2)}) collective-permute-start(bf16[16,2176]{1,0:T(8,128)(2,1)S(1)} %shard_map.112.refs_0_), channel_id=1, source_target_pairs={{0,16},{1,17},{2,18},{3,19},{4,20},{5,21},{6,22},{7,23},{8,24},{9,... | collective-permute-start | bytes 208904 | tf_op jit(solution)/shard_map/ppermute | solution.py:36
  10.4 9.7 %collective-permute-start.1 = (bf16[32,2176]{1,0:T(8,128)(2,1)S(1)}, bf16[32,2176]{1,0:T(8,128)(2,1)S(1)}, u32[]{:S(2)}, u32[]{:S(2)}) collective-permute-start(bf16[32,2176]{1,0:T(8,128)(2,1)S(1)} %shard_map.113.refs_0_), channel_id=1, source_target_pairs={{0,2},{1,3},{2,0},{3,1},{4,6},{5,7},{6,4},{7,5},{8,10},{9,11},{10,... | collective-permute-start | bytes 417800 | tf_op jit(solution)/shard_map/ppermute | solution.py:36
  12.4 9.4 %collective-permute-start.2 = (bf16[32,2176]{1,0:T(8,128)(2,1)S(1)}, bf16[32,2176]{1,0:T(8,128)(2,1)S(1)}, u32[]{:S(2)}, u32[]{:S(2)}) collective-permute-start(bf16[32,2176]{1,0:T(8,128)(2,1)S(1)} %shard_map.113.refs_0_), channel_id=1, source_target_pairs={{0,4},{1,5},{2,6},{3,7},{4,0},{5,1},{6,2},{7,3},{8,12},{9,13},{10,... | collective-permute-start | bytes 417800 | tf_op jit(solution)/shard_map/ppermute | solution.py:36
  14.1 7.7 %collective-permute-start.3 = (bf16[32,2176]{1,0:T(8,128)(2,1)S(1)}, bf16[32,2176]{1,0:T(8,128)(2,1)S(1)}, u32[]{:S(2)}, u32[]{:S(2)}) collective-permute-start(bf16[32,2176]{1,0:T(8,128)(2,1)S(1)} %shard_map.113.refs_0_), channel_id=1, source_target_pairs={{0,6},{1,7},{2,4},{3,5},{4,2},{5,3},{6,0},{7,1},{8,14},{9,15},{10,... | collective-permute-start | bytes 417800 | tf_op jit(solution)/shard_map/ppermute | solution.py:36
  18.2 8.1 %collective-permute-start.12 = (bf16[32,2176]{1,0:T(8,128)(2,1)S(1)}, bf16[32,2176]{1,0:T(8,128)(2,1)S(1)}, u32[]{:S(2)}, u32[]{:S(2)}) collective-permute-start(bf16[32,2176]{1,0:T(8,128)(2,1)S(1)} %shard_map.117.refs_0_), channel_id=1, source_target_pairs={{0,2},{1,3},{2,0},{3,1},{4,6},{5,7},{6,4},{7,5},{8,10},{9,11},{10,... | collective-permute-start | bytes 417800 | tf_op jit(solution)/shard_map/ppermute | solution.py:36
  18.8 8.7 %collective-permute-start.13 = (bf16[32,2176]{1,0:T(8,128)(2,1)S(1)}, bf16[32,2176]{1,0:T(8,128)(2,1)S(1)}, u32[]{:S(2)}, u32[]{:S(2)}) collective-permute-start(bf16[32,2176]{1,0:T(8,128)(2,1)S(1)} %shard_map.117.refs_0_), channel_id=1, source_target_pairs={{0,4},{1,5},{2,6},{3,7},{4,0},{5,1},{6,2},{7,3},{8,12},{9,13},{10,... | collective-permute-start | bytes 417800 | tf_op jit(solution)/shard_map/ppermute | solution.py:36
  20.1 7.9 %collective-permute-start.14 = (bf16[32,2176]{1,0:T(8,128)(2,1)S(1)}, bf16[32,2176]{1,0:T(8,128)(2,1)S(1)}, u32[]{:S(2)}, u32[]{:S(2)}) collective-permute-start(bf16[32,2176]{1,0:T(8,128)(2,1)S(1)} %shard_map.117.refs_0_), channel_id=1, source_target_pairs={{0,6},{1,7},{2,4},{3,5},{4,2},{5,3},{6,0},{7,1},{8,14},{9,15},{10,... | collective-permute-start | bytes 417800 | tf_op jit(solution)/shard_map/ppermute | solution.py:36
  23.5 9.8 %collective-permute-start.6 = (bf16[32,2048]{1,0:T(8,128)(2,1)S(1)}, bf16[32,2048]{1,0:T(8,128)(2,1)S(1)}, u32[]{:S(2)}, u32[]{:S(2)}) collective-permute-start(bf16[32,2048]{1,0:T(8,128)(2,1)S(1)} %get-tuple-element.24), channel_id=1, source_target_pairs={{0,2},{1,3},{2,0},{3,1},{4,6},{5,7},{6,4},{7,5},{8,10},{9,11},{10,... | collective-permute-start | bytes 393224 | tf_op jit(solution)/shard_map/ppermute | solution.py:36
  24.5 8.8 %collective-permute-start.7 = (bf16[32,2048]{1,0:T(8,128)(2,1)S(1)}, bf16[32,2048]{1,0:T(8,128)(2,1)S(1)}, u32[]{:S(2)}, u32[]{:S(2)}) collective-permute-start(bf16[32,2048]{1,0:T(8,128)(2,1)S(1)} %get-tuple-element.25), channel_id=1, source_target_pairs={{0,4},{1,5},{2,6},{3,7},{4,0},{5,1},{6,2},{7,3},{8,12},{9,13},{10,... | collective-permute-start | bytes 393224 | tf_op jit(solution)/shard_map/ppermute | solution.py:36
  26.3 18.4 %copy-start = (s32[1,1,8,8]{3,2,1,0:T(8,128)S(1)}, s32[1,1,8,8]{3,2,1,0:T(8,128)}, u32[]{:S(2)}) copy-start(s32[1,1,8,8]{3,2,1,0:T(8,128)} %param.11) | copy-start | bytes 772
  26.3 18.4 %copy-start.1 = (f32[1,1,8,8]{3,2,1,0:T(8,128)S(1)}, f32[1,1,8,8]{3,2,1,0:T(8,128)}, u32[]{:S(2)}) copy-start(f32[1,1,8,8]{3,2,1,0:T(8,128)} %param.13) | copy-start | bytes 772
  26.3 7.8 %collective-permute-start.8 = (bf16[32,2048]{1,0:T(8,128)(2,1)S(1)}, bf16[32,2048]{1,0:T(8,128)(2,1)S(1)}, u32[]{:S(2)}, u32[]{:S(2)}) collective-permute-start(bf16[32,2048]{1,0:T(8,128)(2,1)S(1)} %get-tuple-element.26), channel_id=1, source_target_pairs={{0,6},{1,7},{2,4},{3,5},{4,2},{5,3},{6,0},{7,1},{8,14},{9,15},{10,... | collective-permute-start | bytes 393224 | tf_op jit(solution)/shard_map/ppermute | solution.py:36
  29.6 7.6 %collective-permute-start.15 = (bf16[32,2048]{1,0:T(8,128)(2,1)S(1)}, bf16[32,2048]{1,0:T(8,128)(2,1)S(1)}, u32[]{:S(2)}, u32[]{:S(2)}) collective-permute-start(bf16[32,2048]{1,0:T(8,128)(2,1)S(1)} %get-tuple-element.31), channel_id=1, source_target_pairs={{0,2},{1,3},{2,0},{3,1},{4,6},{5,7},{6,4},{7,5},{8,10},{9,11},{10,... | collective-permute-start | bytes 393224 | tf_op jit(solution)/shard_map/ppermute | solution.py:36
  30.8 6.4 %collective-permute-start.16 = (bf16[32,2048]{1,0:T(8,128)(2,1)S(1)}, bf16[32,2048]{1,0:T(8,128)(2,1)S(1)}, u32[]{:S(2)}, u32[]{:S(2)}) collective-permute-start(bf16[32,2048]{1,0:T(8,128)(2,1)S(1)} %get-tuple-element.32), channel_id=1, source_target_pairs={{0,4},{1,5},{2,6},{3,7},{4,0},{5,1},{6,2},{7,3},{8,12},{9,13},{10,... | collective-permute-start | bytes 393224 | tf_op jit(solution)/shard_map/ppermute | solution.py:36
  33.3 5.9 %collective-permute-start.17 = (bf16[32,2048]{1,0:T(8,128)(2,1)S(1)}, bf16[32,2048]{1,0:T(8,128)(2,1)S(1)}, u32[]{:S(2)}, u32[]{:S(2)}) collective-permute-start(bf16[32,2048]{1,0:T(8,128)(2,1)S(1)} %get-tuple-element.33), channel_id=1, source_target_pairs={{0,6},{1,7},{2,4},{3,5},{4,2},{5,3},{6,0},{7,1},{8,14},{9,15},{10,... | collective-permute-start | bytes 393224 | tf_op jit(solution)/shard_map/ppermute | solution.py:36
  34.2 7.4 %collective-permute-start.9 = (bf16[16,2048]{1,0:T(8,128)(2,1)S(1)}, bf16[16,2048]{1,0:T(8,128)(2,1)S(1)}, u32[]{:S(2)}, u32[]{:S(2)}) collective-permute-start(bf16[16,2048]{1,0:T(8,128)(2,1)S(1)} %get-tuple-element.27), channel_id=1, source_target_pairs={{0,24},{1,25},{2,26},{3,27},{4,28},{5,29},{6,30},{7,31},{8,16},{9,... | collective-permute-start | bytes 196616 | tf_op jit(solution)/shard_map/ppermute | solution.py:36
  39.2 5.5 %collective-permute-start.18 = (bf16[16,2048]{1,0:T(8,128)(2,1)S(1)}, bf16[16,2048]{1,0:T(8,128)(2,1)S(1)}, u32[]{:S(2)}, u32[]{:S(2)}) collective-permute-start(bf16[16,2048]{1,0:T(8,128)(2,1)S(1)} %get-tuple-element.34), channel_id=1, source_target_pairs={{0,16},{1,17},{2,18},{3,19},{4,20},{5,21},{6,22},{7,23},{8,24},{9,... | collective-permute-start | bytes 196616 | tf_op jit(solution)/shard_map/ppermute | solution.py:36
  39.7 5.0 %collective-permute-start.19 = (bf16[16,2048]{1,0:T(8,128)(2,1)S(1)}, bf16[16,2048]{1,0:T(8,128)(2,1)S(1)}, u32[]{:S(2)}, u32[]{:S(2)}) collective-permute-start(bf16[16,2048]{1,0:T(8,128)(2,1)S(1)} %get-tuple-element.35), channel_id=1, source_target_pairs={{0,8},{1,9},{2,10},{3,11},{4,12},{5,13},{6,14},{7,15},{8,0},{9,1},... | collective-permute-start | bytes 196616 | tf_op jit(solution)/shard_map/ppermute | solution.py:36
where the time goes:
time: 56.5 us; the launch traced here: 56.3 us
  starting transfers between devices  28.3 us (50%)
  blocking collectives  10.3 us (18%)
  waiting for transfers between devices  8.76 us (16%)
  Pallas kernels  8.17 us (14%)
  between operations  0.73 us (1%)
    ppermute x20, starting transfers between devices, exclusive(): return lax.ppermute(value, 'expert', pairs)  28.3 us
    all_to_all x1, blocking collectives, on_device(): lax.all_to_all(terms, 'expert', split_axis=0, concat_axis=0, tiled=True)  10.3 us
    ppermute x20, waiting for transfers between devices, exclusive(): return lax.ppermute(value, 'expert', pairs)  8.76 us
    pallas_call x10, Pallas kernels, run_kernel(): pl.pallas_call(body, out_shape=outs, in_specs=[pl.BlockSpec(memory_space=...  8.17 us
  transfers between devices with their start and end apart: 20, of which 6 were waited for; matrix products, arithmetic and copies ran while one was open for 0% of the time, Pallas kernels for 12%

commit v1 on v0

--- a/solution.py
+++ b/solution.py
@@ -293,7 +293,7 @@
         for stream, layers in enumerate(streams):
             joined = join_rows([column[j] for j in layers])
             if stream == 1:
-                joined = after(joined, own, other_in, other_out)
+                joined = after(joined, other_in, other_out)
             block = [joined]
             for mask in inner_masks:
                 block.append(exclusive(joined, mask))

time: 56.5 us -> 56.8 us (level)
  waiting for transfers between devices: 8.76 us -> 11.1 us
  starting transfers between devices: 28.3 us -> 27 us
  blocking collectives: 10.3 us -> 9.6 us
    ppermute x20, waiting for transfers between devices: 8.76 us -> 11.1 us  [exclusive(): return lax.ppermute(value, 'expert', pairs)]
    ppermute x20, starting transfers between devices: 28.3 us -> 27 us  [exclusive(): return lax.ppermute(value, 'expert', pairs)]
    all_to_all x1, blocking collectives: 10.3 us -> 9.6 us  [on_device(): lax.all_to_all(terms, 'expert', split_axis=0, concat_axis=0, tiled=True)]
  transfers between devices with their start and end apart: 20 -> 20, of which waited for: 6 -> 9; matrix products, arithmetic and copies ran while one was open for 0% -> 0% of each run, Pallas kernels for 12% -> 12%
where the time goes in v1:
time: 56.8 us; the launch traced here: 56.6 us
  starting transfers between devices  27 us (48%)
  waiting for transfers between devices  11.1 us (20%)
  blocking collectives  9.6 us (17%)
  Pallas kernels  8.16 us (14%)
  between operations  0.75 us (1%)
    ppermute x20, starting transfers between devices, exclusive(): return lax.ppermute(value, 'expert', pairs)  27 us
    ppermute x20, waiting for transfers between devices, exclusive(): return lax.ppermute(value, 'expert', pairs)  11.1 us
    all_to_all x1, blocking collectives, on_device(): lax.all_to_all(terms, 'expert', split_axis=0, concat_axis=0, tiled=True)  9.6 us
    pallas_call x10, Pallas kernels, run_kernel(): pl.pallas_call(body, out_shape=outs, in_specs=[pl.BlockSpec(memory_space=...  8.16 us
  transfers between devices with their start and end apart: 20, of which 9 were waited for; matrix products, arithmetic and copies ran while one was open for 0% of the time, Pallas kernels for 12%

profile of v1, /device:TPU:0, one launch (start us, length us, event | category | flops | bytes accessed | tf_op | source)
XLA Modules:
  0.0 56.6 jit_solution(2864778085168348379)
XLA Ops:
  0.6 0.5 collective-permute-start.4
  1.1 0.1 collective-permute-start.5
  1.2 1.1 %shard_map.112.refs_0_ = bf16[16,2176]{1,0:T(8,128)(2,1)S(1)} custom-call(bf16[8,2048]{1,0:T(8,128)(2,1)} %bitcast.24, bf16[8,2048]{1,0:T(8,128)(2,1)} %bitcast.25, s32[8,8]{1,0:T(8,128)} %bitcast.15, s32[8,8]{1,0:T(8,128)} %bitcast.26, f32[8,8]{1,0:T(8,128)} %bitcast.17, f32[8,8]{1,0:T(8,128)} %bitcast.27, s32[1,16]{1,0:T(1,128)} %refs_6_.1), custom_call_target="tpu_custom_call" | custom-call | tf_op jit(solution)/shard_map/pallas_call | solution.py:16
  2.3 5.1 %collective-permute-start = (bf16[16,2176]{1,0:T(8,128)(2,1)S(1)}, bf16[16,2176]{1,0:T(8,128)(2,1)S(1)}, u32[]{:S(2)}, u32[]{:S(2)}) collective-permute-start(bf16[16,2176]{1,0:T(8,128)(2,1)S(1)} %shard_map.112.refs_0_), channel_id=1, source_target_pairs={{0,24},{1,25},{2,26},{3,27},{4,28},{5,29},{6,30},{7,31},{8,16},{9,... | collective-permute-start | bytes 208904 | tf_op jit(solution)/shard_map/ppermute | solution.py:36
  7.4 0.0 collective-permute-start.10
  7.4 0.6 %collective-permute-start.11 = (bf16[16,2176]{1,0:T(8,128)(2,1)S(1)}, bf16[16,2176]{1,0:T(8,128)(2,1)S(1)}, u32[]{:S(2)}, u32[]{:S(2)}) collective-permute-start(bf16[16,2176]{1,0:T(8,128)(2,1)S(1)} %shard_map.112.refs_0_), channel_id=1, source_target_pairs={{0,16},{1,17},{2,18},{3,19},{4,20},{5,21},{6,22},{7,23},{8,24},{9,... | collective-permute-start | bytes 208904 | tf_op jit(solution)/shard_map/ppermute | solution.py:36
  8.1 2.3 %collective-permute-done.refs_1_ = bf16[16,2176]{1,0:T(8,128)(2,1)S(1)} collective-permute-done((bf16[16,2176]{1,0:T(8,128)(2,1)S(1)}, bf16[16,2176]{1,0:T(8,128)(2,1)S(1)}, u32[]{:S(2)}, u32[]{:S(2)}) %collective-permute-start) | collective-permute-done | bytes 69664 | tf_op jit(solution)/shard_map/ppermute | solution.py:36
  10.4 1.8 %collective-permute-start.1 = (bf16[32,2176]{1,0:T(8,128)(2,1)S(1)}, bf16[32,2176]{1,0:T(8,128)(2,1)S(1)}, u32[]{:S(2)}, u32[]{:S(2)}) collective-permute-start(bf16[32,2176]{1,0:T(8,128)(2,1)S(1)} %shard_map.113.refs_0_), channel_id=1, source_target_pairs={{0,2},{1,3},{2,0},{3,1},{4,6},{5,7},{6,4},{7,5},{8,10},{9,11},{10,... | collective-permute-start | bytes 417800 | tf_op jit(solution)/shard_map/ppermute | solution.py:36
  12.3 0.2 collective-permute-done.10.refs_0_
  12.4 1.6 %collective-permute-start.2 = (bf16[32,2176]{1,0:T(8,128)(2,1)S(1)}, bf16[32,2176]{1,0:T(8,128)(2,1)S(1)}, u32[]{:S(2)}, u32[]{:S(2)}) collective-permute-start(bf16[32,2176]{1,0:T(8,128)(2,1)S(1)} %shard_map.113.refs_0_), channel_id=1, source_target_pairs={{0,4},{1,5},{2,6},{3,7},{4,0},{5,1},{6,2},{7,3},{8,12},{9,13},{10,... | collective-permute-start | bytes 417800 | tf_op jit(solution)/shard_map/ppermute | solution.py:36
  14.1 0.0 collective-permute-done.11.refs_1_
  14.1 1.7 %collective-permute-start.3 = (bf16[32,2176]{1,0:T(8,128)(2,1)S(1)}, bf16[32,2176]{1,0:T(8,128)(2,1)S(1)}, u32[]{:S(2)}, u32[]{:S(2)}) collective-permute-start(bf16[32,2176]{1,0:T(8,128)(2,1)S(1)} %shard_map.113.refs_0_), channel_id=1, source_target_pairs={{0,6},{1,7},{2,4},{3,5},{4,2},{5,3},{6,0},{7,1},{8,14},{9,15},{10,... | collective-permute-start | bytes 417800 | tf_op jit(solution)/shard_map/ppermute | solution.py:36
  15.8 0.0 collective-permute-done.5.refs_7_
  15.9 0.0 collective-permute-done.4.refs_5_
  15.9 0.6 %collective-permute-start.12 = (bf16[32,2176]{1,0:T(8,128)(2,1)S(1)}, bf16[32,2176]{1,0:T(8,128)(2,1)S(1)}, u32[]{:S(2)}, u32[]{:S(2)}) collective-permute-start(bf16[32,2176]{1,0:T(8,128)(2,1)S(1)} %shard_map.117.refs_0_), channel_id=1, source_target_pairs={{0,2},{1,3},{2,0},{3,1},{4,6},{5,7},{6,4},{7,5},{8,10},{9,11},{10,... | collective-permute-start | bytes 417800 | tf_op jit(solution)/shard_map/ppermute | solution.py:36
  16.5 1.2 %collective-permute-start.13 = (bf16[32,2176]{1,0:T(8,128)(2,1)S(1)}, bf16[32,2176]{1,0:T(8,128)(2,1)S(1)}, u32[]{:S(2)}, u32[]{:S(2)}) collective-permute-start(bf16[32,2176]{1,0:T(8,128)(2,1)S(1)} %shard_map.117.refs_0_), channel_id=1, source_target_pairs={{0,4},{1,5},{2,6},{3,7},{4,0},{5,1},{6,2},{7,3},{8,12},{9,13},{10,... | collective-permute-start | bytes 417800 | tf_op jit(solution)/shard_map/ppermute | solution.py:36
  17.7 0.0 collective-permute-done.1.refs_1_
  17.7 1.7 %collective-permute-start.14 = (bf16[32,2176]{1,0:T(8,128)(2,1)S(1)}, bf16[32,2176]{1,0:T(8,128)(2,1)S(1)}, u32[]{:S(2)}, u32[]{:S(2)}) collective-permute-start(bf16[32,2176]{1,0:T(8,128)(2,1)S(1)} %shard_map.117.refs_0_), channel_id=1, source_target_pairs={{0,6},{1,7},{2,4},{3,5},{4,2},{5,3},{6,0},{7,1},{8,14},{9,15},{10,... | collective-permute-start | bytes 417800 | tf_op jit(solution)/shard_map/ppermute | solution.py:36
  19.4 2.4 %shard_map.114 = (bf16[2048,768]{1,0:T(8,128)(2,1)S(1)}, bf16[384,2048]{1,0:T(8,128)(2,1)S(1)}) custom-call(bf16[2048,768]{1,0:T(8,128)(2,1)} %bitcast.21, bf16[384,2048]{1,0:T(8,128)(2,1)} %bitcast.23), custom_call_target="tpu_custom_call" | custom-call | tf_op jit(solution)/shard_map/pallas_call | solution.py:16
  21.8 0.4 collective-permute-done.2.refs_2_
  22.2 0.0 collective-permute-done.3.refs_3_
  22.2 1.7 %shard_map.115 = (bf16[32,2048]{1,0:T(8,128)(2,1)S(1)}, bf16[32,2048]{1,0:T(8,128)(2,1)S(1)}, bf16[32,2048]{1,0:T(8,128)(2,1)S(1)}, bf16[32,2048]{1,0:T(8,128)(2,1)S(1)}) custom-call(bf16[32,2176]{1,0:T(8,128)(2,1)S(1)} %shard_map.113.refs_0_, bf16[32,2176]{1,0:T(8,128)(2,1)S(1)} %collective-permute-done.1.refs_1_, ...), custom_call_target="tpu_custom_call" | custom-call | tf_op jit(solution)/shard_map/pallas_call | solution.py:16
  23.9 1.7 %collective-permute-start.6 = (bf16[32,2048]{1,0:T(8,128)(2,1)S(1)}, bf16[32,2048]{1,0:T(8,128)(2,1)S(1)}, u32[]{:S(2)}, u32[]{:S(2)}) collective-permute-start(bf16[32,2048]{1,0:T(8,128)(2,1)S(1)} %get-tuple-element.24), channel_id=1, source_target_pairs={{0,2},{1,3},{2,0},{3,1},{4,6},{5,7},{6,4},{7,5},{8,10},{9,11},{10,... | collective-permute-start | bytes 393224 | tf_op jit(solution)/shard_map/ppermute | solution.py:36
  25.6 2.6 %collective-permute-start.7 = (bf16[32,2048]{1,0:T(8,128)(2,1)S(1)}, bf16[32,2048]{1,0:T(8,128)(2,1)S(1)}, u32[]{:S(2)}, u32[]{:S(2)}) collective-permute-start(bf16[32,2048]{1,0:T(8,128)(2,1)S(1)} %get-tuple-element.25), channel_id=1, source_target_pairs={{0,4},{1,5},{2,6},{3,7},{4,0},{5,1},{6,2},{7,3},{8,12},{9,13},{10,... | collective-permute-start | bytes 393224 | tf_op jit(solution)/shard_map/ppermute | solution.py:36
  28.2 0.0 collective-permute-done.12.refs_1_
  28.3 0.0 collective-permute-start.8
  28.3 0.0 collective-permute-done.14.refs_3_
  28.3 1.7 %shard_map.118 = (bf16[32,2048]{1,0:T(8,128)(2,1)S(1)}, bf16[32,2048]{1,0:T(8,128)(2,1)S(1)}, bf16[32,2048]{1,0:T(8,128)(2,1)S(1)}, bf16[32,2048]{1,0:T(8,128)(2,1)S(1)}) custom-call(bf16[32,2176]{1,0:T(8,128)(2,1)S(1)} %shard_map.117.refs_0_, bf16[32,2176]{1,0:T(8,128)(2,1)S(1)} %collective-permute-done.12.refs_1_, ...), custom_call_target="tpu_custom_call" | custom-call | tf_op jit(solution)/shard_map/pallas_call | solution.py:16
  30.0 2.1 %collective-permute-start.15 = (bf16[32,2048]{1,0:T(8,128)(2,1)S(1)}, bf16[32,2048]{1,0:T(8,128)(2,1)S(1)}, u32[]{:S(2)}, u32[]{:S(2)}) collective-permute-start(bf16[32,2048]{1,0:T(8,128)(2,1)S(1)} %get-tuple-element.31), channel_id=1, source_target_pairs={{0,2},{1,3},{2,0},{3,1},{4,6},{5,7},{6,4},{7,5},{8,10},{9,11},{10,... | collective-permute-start | bytes 393224 | tf_op jit(solution)/shard_map/ppermute | solution.py:36
  32.0 1.9 %collective-permute-start.16 = (bf16[32,2048]{1,0:T(8,128)(2,1)S(1)}, bf16[32,2048]{1,0:T(8,128)(2,1)S(1)}, u32[]{:S(2)}, u32[]{:S(2)}) collective-permute-start(bf16[32,2048]{1,0:T(8,128)(2,1)S(1)} %get-tuple-element.32), channel_id=1, source_target_pairs={{0,4},{1,5},{2,6},{3,7},{4,0},{5,1},{6,2},{7,3},{8,12},{9,13},{10,... | collective-permute-start | bytes 393224 | tf_op jit(solution)/shard_map/ppermute | solution.py:36
  33.9 0.0 collective-permute-done.6.refs_1_
  33.9 0.1 collective-permute-start.17
  34.0 0.8 %collective-permute-done.7.refs_2_ = bf16[32,2048]{1,0:T(8,128)(2,1)S(1)} collective-permute-done((bf16[32,2048]{1,0:T(8,128)(2,1)S(1)}, bf16[32,2048]{1,0:T(8,128)(2,1)S(1)}, u32[]{:S(2)}, u32[]{:S(2)}) %collective-permute-start.7) | collective-permute-done | bytes 131104 | tf_op jit(solution)/shard_map/ppermute | solution.py:36
  34.8 0.5 collective-permute-done.8.refs_3_
  35.3 0.1 shard_map.116
  35.4 2.0 %collective-permute-start.9 = (bf16[16,2048]{1,0:T(8,128)(2,1)S(1)}, bf16[16,2048]{1,0:T(8,128)(2,1)S(1)}, u32[]{:S(2)}, u32[]{:S(2)}) collective-permute-start(bf16[16,2048]{1,0:T(8,128)(2,1)S(1)} %get-tuple-element.27), channel_id=1, source_target_pairs={{0,24},{1,25},{2,26},{3,27},{4,28},{5,29},{6,30},{7,31},{8,16},{9,... | collective-permute-start | bytes 196616 | tf_op jit(solution)/shard_map/ppermute | solution.py:36
  37.4 0.0 collective-permute-done.15.refs_1_
  37.4 0.4 collective-permute-done.16.refs_2_
  37.8 1.9 %collective-permute-done.17.refs_3_ = bf16[32,2048]{1,0:T(8,128)(2,1)S(1)} collective-permute-done((bf16[32,2048]{1,0:T(8,128)(2,1)S(1)}, bf16[32,2048]{1,0:T(8,128)(2,1)S(1)}, u32[]{:S(2)}, u32[]{:S(2)}) %collective-permute-start.17) | collective-permute-done | bytes 131104 | tf_op jit(solution)/shard_map/ppermute | solution.py:36
  39.8 0.1 shard_map.119
  39.8 0.1 collective-permute-start.18
  39.9 1.4 %collective-permute-start.19 = (bf16[16,2048]{1,0:T(8,128)(2,1)S(1)}, bf16[16,2048]{1,0:T(8,128)(2,1)S(1)}, u32[]{:S(2)}, u32[]{:S(2)}) collective-permute-start(bf16[16,2048]{1,0:T(8,128)(2,1)S(1)} %get-tuple-element.35), channel_id=1, source_target_pairs={{0,8},{1,9},{2,10},{3,11},{4,12},{5,13},{6,14},{7,15},{8,0},{9,1},... | collective-permute-start | bytes 196616 | tf_op jit(solution)/shard_map/ppermute | solution.py:36
  41.3 0.4 collective-permute-done.9.refs_0_
  41.7 4.0 %collective-permute-done.18.refs_2_ = bf16[16,2048]{1,0:T(8,128)(2,1)S(1)} collective-permute-done((bf16[16,2048]{1,0:T(8,128)(2,1)S(1)}, bf16[16,2048]{1,0:T(8,128)(2,1)S(1)}, u32[]{:S(2)}, u32[]{:S(2)}) %collective-permute-start.18) | collective-permute-done | bytes 65568 | tf_op jit(solution)/shard_map/ppermute | solution.py:36
  45.8 0.0 collective-permute-done.19.refs_3_
  45.8 0.7 %shard_map.120 = (bf16[8,2048]{1,0:T(8,128)(2,1)}, bf16[8,2048]{1,0:T(8,128)(2,1)}, f32[32,16]{1,0:T(8,128)S(1)}) custom-call(bf16[16,2048]{1,0:T(8,128)(2,1)S(1)} %collective-permute-done.9.refs_0_, f32[16,2048]{1,0:T(8,128)S(1)} %get-tuple-element.28.refs_1_, bf16[16,2048]{1,0:T(8,128)(2,1)S(1)} %collective-permute-done.18.refs_2_, ...), custom_call_target="tpu_custom_call" | custom-call | tf_op jit(solution)/shard_map/pallas_call | solution.py:16
  46.4 9.6 %all_to_all.11 = f32[32,1,16]{2,1,0:T(1,128)S(1)} all-to-all(f32[32,1,16]{2,1,0:T(1,128)S(1)} %bitcast.19), channel_id=1, replica_groups=mesh['section'=1,'expert'=32] {'expert'}, dimensions={0} | all-to-all | bytes 4096 | tf_op jit(solution)/shard_map/all_to_all | solution.py:334
  56.0 0.5 shard_map.121
  (7 shorter events, 0.0 us)
Async XLA Ops:
  0.6 15.2 %collective-permute-start.4 = (bf16[2048,768]{1,0:T(8,128)(2,1)}, bf16[2048,768]{1,0:T(8,128)(2,1)S(1)}, u32[]{:S(2)}, u32[]{:S(2)}) collective-permute-start(bf16[2048,768]{1,0:T(8,128)(2,1)} %bitcast.20), channel_id=1, source_target_pairs={{0,1},{1,0},{2,3},{3,2},{4,5},{5,4},{6,7},{7,6},{8,9},{9,8},{10,11... | collective-permute-start | bytes 9437192 | tf_op jit(solution)/shard_map/ppermute | solution.py:36
  1.1 14.7 %collective-permute-start.5 = (bf16[384,2048]{1,0:T(8,128)(2,1)}, bf16[384,2048]{1,0:T(8,128)(2,1)S(1)}, u32[]{:S(2)}, u32[]{:S(2)}) collective-permute-start(bf16[384,2048]{1,0:T(8,128)(2,1)} %bitcast.22), channel_id=1, source_target_pairs={{0,1},{1,0},{2,3},{3,2},{4,5},{5,4},{6,7},{7,6},{8,9},{9,8},{10,11... | collective-permute-start | bytes 4718600 | tf_op jit(solution)/shard_map/ppermute | solution.py:36
  2.3 8.1 %collective-permute-start = (bf16[16,2176]{1,0:T(8,128)(2,1)S(1)}, bf16[16,2176]{1,0:T(8,128)(2,1)S(1)}, u32[]{:S(2)}, u32[]{:S(2)}) collective-permute-start(bf16[16,2176]{1,0:T(8,128)(2,1)S(1)} %shard_map.112.refs_0_), channel_id=1, source_target_pairs={{0,24},{1,25},{2,26},{3,27},{4,28},{5,29},{6,30},{7,31},{8,16},{9,... | collective-permute-start | bytes 208904 | tf_op jit(solution)/shard_map/ppermute | solution.py:36
  7.4 5.0 %collective-permute-start.10 = (bf16[16,2176]{1,0:T(8,128)(2,1)S(1)}, bf16[16,2176]{1,0:T(8,128)(2,1)S(1)}, u32[]{:S(2)}, u32[]{:S(2)}) collective-permute-start(bf16[16,2176]{1,0:T(8,128)(2,1)S(1)} %shard_map.112.refs_0_), channel_id=1, source_target_pairs={{0,8},{1,9},{2,10},{3,11},{4,12},{5,13},{6,14},{7,15},{8,0},{9,1},... | collective-permute-start | bytes 208904 | tf_op jit(solution)/shard_map/ppermute | solution.py:36
  7.4 6.7 %collective-permute-start.11 = (bf16[16,2176]{1,0:T(8,128)(2,1)S(1)}, bf16[16,2176]{1,0:T(8,128)(2,1)S(1)}, u32[]{:S(2)}, u32[]{:S(2)}) collective-permute-start(bf16[16,2176]{1,0:T(8,128)(2,1)S(1)} %shard_map.112.refs_0_), channel_id=1, source_target_pairs={{0,16},{1,17},{2,18},{3,19},{4,20},{5,21},{6,22},{7,23},{8,24},{9,... | collective-permute-start | bytes 208904 | tf_op jit(solution)/shard_map/ppermute | solution.py:36
  10.4 7.3 %collective-permute-start.1 = (bf16[32,2176]{1,0:T(8,128)(2,1)S(1)}, bf16[32,2176]{1,0:T(8,128)(2,1)S(1)}, u32[]{:S(2)}, u32[]{:S(2)}) collective-permute-start(bf16[32,2176]{1,0:T(8,128)(2,1)S(1)} %shard_map.113.refs_0_), channel_id=1, source_target_pairs={{0,2},{1,3},{2,0},{3,1},{4,6},{5,7},{6,4},{7,5},{8,10},{9,11},{10,... | collective-permute-start | bytes 417800 | tf_op jit(solution)/shard_map/ppermute | solution.py:36
  12.4 9.7 %collective-permute-start.2 = (bf16[32,2176]{1,0:T(8,128)(2,1)S(1)}, bf16[32,2176]{1,0:T(8,128)(2,1)S(1)}, u32[]{:S(2)}, u32[]{:S(2)}) collective-permute-start(bf16[32,2176]{1,0:T(8,128)(2,1)S(1)} %shard_map.113.refs_0_), channel_id=1, source_target_pairs={{0,4},{1,5},{2,6},{3,7},{4,0},{5,1},{6,2},{7,3},{8,12},{9,13},{10,... | collective-permute-start | bytes 417800 | tf_op jit(solution)/shard_map/ppermute | solution.py:36
  14.1 8.1 %collective-permute-start.3 = (bf16[32,2176]{1,0:T(8,128)(2,1)S(1)}, bf16[32,2176]{1,0:T(8,128)(2,1)S(1)}, u32[]{:S(2)}, u32[]{:S(2)}) collective-permute-start(bf16[32,2176]{1,0:T(8,128)(2,1)S(1)} %shard_map.113.refs_0_), channel_id=1, source_target_pairs={{0,6},{1,7},{2,4},{3,5},{4,2},{5,3},{6,0},{7,1},{8,14},{9,15},{10,... | collective-permute-start | bytes 417800 | tf_op jit(solution)/shard_map/ppermute | solution.py:36
  15.9 12.4 %collective-permute-start.12 = (bf16[32,2176]{1,0:T(8,128)(2,1)S(1)}, bf16[32,2176]{1,0:T(8,128)(2,1)S(1)}, u32[]{:S(2)}, u32[]{:S(2)}) collective-permute-start(bf16[32,2176]{1,0:T(8,128)(2,1)S(1)} %shard_map.117.refs_0_), channel_id=1, source_target_pairs={{0,2},{1,3},{2,0},{3,1},{4,6},{5,7},{6,4},{7,5},{8,10},{9,11},{10,... | collective-permute-start | bytes 417800 | tf_op jit(solution)/shard_map/ppermute | solution.py:36
  16.5 11.8 %collective-permute-start.13 = (bf16[32,2176]{1,0:T(8,128)(2,1)S(1)}, bf16[32,2176]{1,0:T(8,128)(2,1)S(1)}, u32[]{:S(2)}, u32[]{:S(2)}) collective-permute-start(bf16[32,2176]{1,0:T(8,128)(2,1)S(1)} %shard_map.117.refs_0_), channel_id=1, source_target_pairs={{0,4},{1,5},{2,6},{3,7},{4,0},{5,1},{6,2},{7,3},{8,12},{9,13},{10,... | collective-permute-start | bytes 417800 | tf_op jit(solution)/shard_map/ppermute | solution.py:36
  17.7 10.6 %collective-permute-start.14 = (bf16[32,2176]{1,0:T(8,128)(2,1)S(1)}, bf16[32,2176]{1,0:T(8,128)(2,1)S(1)}, u32[]{:S(2)}, u32[]{:S(2)}) collective-permute-start(bf16[32,2176]{1,0:T(8,128)(2,1)S(1)} %shard_map.117.refs_0_), channel_id=1, source_target_pairs={{0,6},{1,7},{2,4},{3,5},{4,2},{5,3},{6,0},{7,1},{8,14},{9,15},{10,... | collective-permute-start | bytes 417800 | tf_op jit(solution)/shard_map/ppermute | solution.py:36
  23.9 10.0 %collective-permute-start.6 = (bf16[32,2048]{1,0:T(8,128)(2,1)S(1)}, bf16[32,2048]{1,0:T(8,128)(2,1)S(1)}, u32[]{:S(2)}, u32[]{:S(2)}) collective-permute-start(bf16[32,2048]{1,0:T(8,128)(2,1)S(1)} %get-tuple-element.24), channel_id=1, source_target_pairs={{0,2},{1,3},{2,0},{3,1},{4,6},{5,7},{6,4},{7,5},{8,10},{9,11},{10,... | collective-permute-start | bytes 393224 | tf_op jit(solution)/shard_map/ppermute | solution.py:36
  25.6 9.2 %collective-permute-start.7 = (bf16[32,2048]{1,0:T(8,128)(2,1)S(1)}, bf16[32,2048]{1,0:T(8,128)(2,1)S(1)}, u32[]{:S(2)}, u32[]{:S(2)}) collective-permute-start(bf16[32,2048]{1,0:T(8,128)(2,1)S(1)} %get-tuple-element.25), channel_id=1, source_target_pairs={{0,4},{1,5},{2,6},{3,7},{4,0},{5,1},{6,2},{7,3},{8,12},{9,13},{10,... | collective-permute-start | bytes 393224 | tf_op jit(solution)/shard_map/ppermute | solution.py:36
  28.3 17.5 %copy-start = (s32[1,1,8,8]{3,2,1,0:T(8,128)S(1)}, s32[1,1,8,8]{3,2,1,0:T(8,128)}, u32[]{:S(2)}) copy-start(s32[1,1,8,8]{3,2,1,0:T(8,128)} %param.11) | copy-start | bytes 772
  28.3 17.5 %copy-start.1 = (f32[1,1,8,8]{3,2,1,0:T(8,128)S(1)}, f32[1,1,8,8]{3,2,1,0:T(8,128)}, u32[]{:S(2)}) copy-start(f32[1,1,8,8]{3,2,1,0:T(8,128)} %param.13) | copy-start | bytes 772
  28.3 7.1 %collective-permute-start.8 = (bf16[32,2048]{1,0:T(8,128)(2,1)S(1)}, bf16[32,2048]{1,0:T(8,128)(2,1)S(1)}, u32[]{:S(2)}, u32[]{:S(2)}) collective-permute-start(bf16[32,2048]{1,0:T(8,128)(2,1)S(1)} %get-tuple-element.26), channel_id=1, source_target_pairs={{0,6},{1,7},{2,4},{3,5},{4,2},{5,3},{6,0},{7,1},{8,14},{9,15},{10,... | collective-permute-start | bytes 393224 | tf_op jit(solution)/shard_map/ppermute | solution.py:36
  30.0 7.4 %collective-permute-start.15 = (bf16[32,2048]{1,0:T(8,128)(2,1)S(1)}, bf16[32,2048]{1,0:T(8,128)(2,1)S(1)}, u32[]{:S(2)}, u32[]{:S(2)}) collective-permute-start(bf16[32,2048]{1,0:T(8,128)(2,1)S(1)} %get-tuple-element.31), channel_id=1, source_target_pairs={{0,2},{1,3},{2,0},{3,1},{4,6},{5,7},{6,4},{7,5},{8,10},{9,11},{10,... | collective-permute-start | bytes 393224 | tf_op jit(solution)/shard_map/ppermute | solution.py:36
  32.0 5.8 %collective-permute-start.16 = (bf16[32,2048]{1,0:T(8,128)(2,1)S(1)}, bf16[32,2048]{1,0:T(8,128)(2,1)S(1)}, u32[]{:S(2)}, u32[]{:S(2)}) collective-permute-start(bf16[32,2048]{1,0:T(8,128)(2,1)S(1)} %get-tuple-element.32), channel_id=1, source_target_pairs={{0,4},{1,5},{2,6},{3,7},{4,0},{5,1},{6,2},{7,3},{8,12},{9,13},{10,... | collective-permute-start | bytes 393224 | tf_op jit(solution)/shard_map/ppermute | solution.py:36
  33.9 5.9 %collective-permute-start.17 = (bf16[32,2048]{1,0:T(8,128)(2,1)S(1)}, bf16[32,2048]{1,0:T(8,128)(2,1)S(1)}, u32[]{:S(2)}, u32[]{:S(2)}) collective-permute-start(bf16[32,2048]{1,0:T(8,128)(2,1)S(1)} %get-tuple-element.33), channel_id=1, source_target_pairs={{0,6},{1,7},{2,4},{3,5},{4,2},{5,3},{6,0},{7,1},{8,14},{9,15},{10,... | collective-permute-start | bytes 393224 | tf_op jit(solution)/shard_map/ppermute | solution.py:36
  35.4 6.3 %collective-permute-start.9 = (bf16[16,2048]{1,0:T(8,128)(2,1)S(1)}, bf16[16,2048]{1,0:T(8,128)(2,1)S(1)}, u32[]{:S(2)}, u32[]{:S(2)}) collective-permute-start(bf16[16,2048]{1,0:T(8,128)(2,1)S(1)} %get-tuple-element.27), channel_id=1, source_target_pairs={{0,24},{1,25},{2,26},{3,27},{4,28},{5,29},{6,30},{7,31},{8,16},{9,... | collective-permute-start | bytes 196616 | tf_op jit(solution)/shard_map/ppermute | solution.py:36
  39.8 5.9 %collective-permute-start.18 = (bf16[16,2048]{1,0:T(8,128)(2,1)S(1)}, bf16[16,2048]{1,0:T(8,128)(2,1)S(1)}, u32[]{:S(2)}, u32[]{:S(2)}) collective-permute-start(bf16[16,2048]{1,0:T(8,128)(2,1)S(1)} %get-tuple-element.34), channel_id=1, source_target_pairs={{0,16},{1,17},{2,18},{3,19},{4,20},{5,21},{6,22},{7,23},{8,24},{9,... | collective-permute-start | bytes 196616 | tf_op jit(solution)/shard_map/ppermute | solution.py:36
  39.9 5.9 %collective-permute-start.19 = (bf16[16,2048]{1,0:T(8,128)(2,1)S(1)}, bf16[16,2048]{1,0:T(8,128)(2,1)S(1)}, u32[]{:S(2)}, u32[]{:S(2)}) collective-permute-start(bf16[16,2048]{1,0:T(8,128)(2,1)S(1)} %get-tuple-element.35), channel_id=1, source_target_pairs={{0,8},{1,9},{2,10},{3,11},{4,12},{5,13},{6,14},{7,15},{8,0},{9,1},... | collective-permute-start | bytes 196616 | tf_op jit(solution)/shard_map/ppermute | solution.py:36

commit v2 on v0

--- a/solution.py
+++ b/solution.py
@@ -61,13 +61,11 @@
         copy.start()
     for copy in copies:
         copy.wait()
-    so_ref, sp_ref, io_ref, ip_ref, go_ref, gp_ref, keep_ref = held
-    model_width = so_ref.shape[1]
+    states_ref, io_ref, ip_ref, go_ref, gp_ref, keep_ref = held
+    model_width = states_ref.shape[1]
     extra = out_ref.shape[1] - model_width
     experts = keep_ref.shape[1]
-    states = jnp.concatenate(
-        [so_ref[...].astype(jnp.float32), sp_ref[...].astype(jnp.float32)], axis=0
-    )
+    states = states_ref[...].astype(jnp.float32)
     out_ref[:, :model_width] = normalize_rows(states).astype(jnp.bfloat16)
     dense_orig = dense_weights(io_ref[...], go_ref[...], experts)
     dense_pruned = dense_weights(ip_ref[...], gp_ref[...], experts)
@@ -267,8 +265,7 @@
             state_pruned = jnp.where(section_index == 0, state_pruned, carry[1])
         picked_orig, weight_orig = item(ids_orig[0]), item(gates_orig[0])
         operands = [
-            state_orig,
-            state_pruned,
+            jnp.concatenate([state_orig, state_pruned], axis=0),
             picked_orig,
             item(ids_pruned[0]),
             weight_orig,
@@ -278,7 +275,7 @@
         packed = run_kernel(
             functools.partial(pack_kernel, len(operands)),
             like(rows, model_width + extra),
-            [in_hbm(value) for value in operands],
+            operands[:1] + [in_hbm(value) for value in operands[1:]],
             [pltpu.VMEM(value.shape, value.dtype) for value in operands]
             + [pltpu.SemaphoreType.DMA((len(operands),))],
             space=pl.ANY,

time: 56.5 us -> 57.3 us (1.014)
  other arithmetic: 0 us -> 0.78 us
    concatenate x0 -> x1, other arithmetic: none -> 0.78 us  [on_device(): jnp.concatenate([state_orig, state_pruned], axis=0)]
  transfers between devices with their start and end apart: 20 -> 20, of which waited for: 6 -> 6; matrix products, arithmetic and copies ran while one was open for 0% -> 1% of each run, Pallas kernels for 12% -> 12%
where the time goes in v2:
time: 57.3 us; the launch traced here: 57.1 us
  starting transfers between devices  28.3 us (49%)
  blocking collectives  10.3 us (18%)
  waiting for transfers between devices  8.77 us (15%)
  Pallas kernels  8.18 us (14%)
  other arithmetic  0.78 us (1%)
  between operations  0.72 us (1%)
    ppermute x20, starting transfers between devices, exclusive(): return lax.ppermute(value, 'expert', pairs)  28.3 us
    all_to_all x1, blocking collectives, on_device(): lax.all_to_all(terms, 'expert', split_axis=0, concat_axis=0, tiled=True)  10.3 us
    ppermute x20, waiting for transfers between devices, exclusive(): return lax.ppermute(value, 'expert', pairs)  8.77 us
    pallas_call x10, Pallas kernels, run_kernel(): pl.pallas_call(body, out_shape=outs, in_specs=[pl.BlockSpec(memory_space=...  8.18 us
  transfers between devices with their start and end apart: 20, of which 6 were waited for; matrix products, arithmetic and copies ran while one was open for 1% of the time, Pallas kernels for 12%

profile of v2, /device:TPU:0, one launch (start us, length us, event | category | flops | bytes accessed | tf_op | source)
XLA Modules:
  0.0 57.1 jit_solution(6995035362464735604)
XLA Ops:
  0.6 0.5 collective-permute-start.4
  1.1 0.1 collective-permute-start.5
  1.2 0.8 %pad_maximum_fusion.refs_0_ = bf16[16,2048]{1,0:T(8,128)(2,1)S(1)} fusion(bf16[8,2048]{1,0:T(8,128)(2,1)} %bitcast.24, bf16[8,2048]{1,0:T(8,128)(2,1)} %bitcast.25), kind=kLoop, calls=%fused_computation | loop fusion | flops 131072 | bytes 131072 | tf_op jit(solution)/shard_map/concatenate | solution.py:268
  2.0 1.1 %shard_map.112.refs_0_ = bf16[16,2176]{1,0:T(8,128)(2,1)S(1)} custom-call(bf16[16,2048]{1,0:T(8,128)(2,1)S(1)} %pad_maximum_fusion.refs_0_, s32[8,8]{1,0:T(8,128)} %bitcast.15, s32[8,8]{1,0:T(8,128)} %bitcast.26, f32[8,8]{1,0:T(8,128)} %bitcast.17, f32[8,8]{1,0:T(8,128)} %bitcast.27, s32[1,16]{1,0:T(1,128)} %refs_5_.1), custom_call_target="tpu_custom_call" | custom-call | tf_op jit(solution)/shard_map/pallas_call | solution.py:16
  3.1 5.1 %collective-permute-start = (bf16[16,2176]{1,0:T(8,128)(2,1)S(1)}, bf16[16,2176]{1,0:T(8,128)(2,1)S(1)}, u32[]{:S(2)}, u32[]{:S(2)}) collective-permute-start(bf16[16,2176]{1,0:T(8,128)(2,1)S(1)} %shard_map.112.refs_0_), channel_id=1, source_target_pairs={{0,24},{1,25},{2,26},{3,27},{4,28},{5,29},{6,30},{7,31},{8,16},{9,... | collective-permute-start | bytes 208904 | tf_op jit(solution)/shard_map/ppermute | solution.py:36
  8.2 0.0 collective-permute-start.10
  8.2 0.6 %collective-permute-start.11 = (bf16[16,2176]{1,0:T(8,128)(2,1)S(1)}, bf16[16,2176]{1,0:T(8,128)(2,1)S(1)}, u32[]{:S(2)}, u32[]{:S(2)}) collective-permute-start(bf16[16,2176]{1,0:T(8,128)(2,1)S(1)} %shard_map.112.refs_0_), channel_id=1, source_target_pairs={{0,16},{1,17},{2,18},{3,19},{4,20},{5,21},{6,22},{7,23},{8,24},{9,... | collective-permute-start | bytes 208904 | tf_op jit(solution)/shard_map/ppermute | solution.py:36
  8.8 2.3 %collective-permute-done.refs_1_ = bf16[16,2176]{1,0:T(8,128)(2,1)S(1)} collective-permute-done((bf16[16,2176]{1,0:T(8,128)(2,1)S(1)}, bf16[16,2176]{1,0:T(8,128)(2,1)S(1)}, u32[]{:S(2)}, u32[]{:S(2)}) %collective-permute-start) | collective-permute-done | bytes 69664 | tf_op jit(solution)/shard_map/ppermute | solution.py:36
  11.2 1.8 %collective-permute-start.1 = (bf16[32,2176]{1,0:T(8,128)(2,1)S(1)}, bf16[32,2176]{1,0:T(8,128)(2,1)S(1)}, u32[]{:S(2)}, u32[]{:S(2)}) collective-permute-start(bf16[32,2176]{1,0:T(8,128)(2,1)S(1)} %shard_map.113.refs_0_), channel_id=1, source_target_pairs={{0,2},{1,3},{2,0},{3,1},{4,6},{5,7},{6,4},{7,5},{8,10},{9,11},{10,... | collective-permute-start | bytes 417800 | tf_op jit(solution)/shard_map/ppermute | solution.py:36
  13.0 0.2 collective-permute-done.10.refs_0_
  13.2 1.6 %collective-permute-start.2 = (bf16[32,2176]{1,0:T(8,128)(2,1)S(1)}, bf16[32,2176]{1,0:T(8,128)(2,1)S(1)}, u32[]{:S(2)}, u32[]{:S(2)}) collective-permute-start(bf16[32,2176]{1,0:T(8,128)(2,1)S(1)} %shard_map.113.refs_0_), channel_id=1, source_target_pairs={{0,4},{1,5},{2,6},{3,7},{4,0},{5,1},{6,2},{7,3},{8,12},{9,13},{10,... | collective-permute-start | bytes 417800 | tf_op jit(solution)/shard_map/ppermute | solution.py:36
  14.9 0.0 collective-permute-done.11.refs_1_
  14.9 1.7 %collective-permute-start.3 = (bf16[32,2176]{1,0:T(8,128)(2,1)S(1)}, bf16[32,2176]{1,0:T(8,128)(2,1)S(1)}, u32[]{:S(2)}, u32[]{:S(2)}) collective-permute-start(bf16[32,2176]{1,0:T(8,128)(2,1)S(1)} %shard_map.113.refs_0_), channel_id=1, source_target_pairs={{0,6},{1,7},{2,4},{3,5},{4,2},{5,3},{6,0},{7,1},{8,14},{9,15},{10,... | collective-permute-start | bytes 417800 | tf_op jit(solution)/shard_map/ppermute | solution.py:36
  16.6 2.4 %shard_map.114 = (bf16[2048,768]{1,0:T(8,128)(2,1)S(1)}, bf16[384,2048]{1,0:T(8,128)(2,1)S(1)}) custom-call(bf16[2048,768]{1,0:T(8,128)(2,1)} %bitcast.21, bf16[384,2048]{1,0:T(8,128)(2,1)} %bitcast.23), custom_call_target="tpu_custom_call" | custom-call | tf_op jit(solution)/shard_map/pallas_call | solution.py:16
  19.0 0.0 collective-permute-done.5.refs_7_
  19.0 0.0 collective-permute-done.4.refs_5_
  19.0 0.6 %collective-permute-start.12 = (bf16[32,2176]{1,0:T(8,128)(2,1)S(1)}, bf16[32,2176]{1,0:T(8,128)(2,1)S(1)}, u32[]{:S(2)}, u32[]{:S(2)}) collective-permute-start(bf16[32,2176]{1,0:T(8,128)(2,1)S(1)} %shard_map.117.refs_0_), channel_id=1, source_target_pairs={{0,2},{1,3},{2,0},{3,1},{4,6},{5,7},{6,4},{7,5},{8,10},{9,11},{10,... | collective-permute-start | bytes 417800 | tf_op jit(solution)/shard_map/ppermute | solution.py:36
  19.6 1.2 %collective-permute-start.13 = (bf16[32,2176]{1,0:T(8,128)(2,1)S(1)}, bf16[32,2176]{1,0:T(8,128)(2,1)S(1)}, u32[]{:S(2)}, u32[]{:S(2)}) collective-permute-start(bf16[32,2176]{1,0:T(8,128)(2,1)S(1)} %shard_map.117.refs_0_), channel_id=1, source_target_pairs={{0,4},{1,5},{2,6},{3,7},{4,0},{5,1},{6,2},{7,3},{8,12},{9,13},{10,... | collective-permute-start | bytes 417800 | tf_op jit(solution)/shard_map/ppermute | solution.py:36
  20.9 0.0 collective-permute-done.1.refs_1_
  20.9 1.7 %collective-permute-start.14 = (bf16[32,2176]{1,0:T(8,128)(2,1)S(1)}, bf16[32,2176]{1,0:T(8,128)(2,1)S(1)}, u32[]{:S(2)}, u32[]{:S(2)}) collective-permute-start(bf16[32,2176]{1,0:T(8,128)(2,1)S(1)} %shard_map.117.refs_0_), channel_id=1, source_target_pairs={{0,6},{1,7},{2,4},{3,5},{4,2},{5,3},{6,0},{7,1},{8,14},{9,15},{10,... | collective-permute-start | bytes 417800 | tf_op jit(solution)/shard_map/ppermute | solution.py:36
  22.6 0.0 collective-permute-done.2.refs_2_
  22.6 0.0 collective-permute-done.3.refs_3_
  22.6 1.7 %shard_map.115 = (bf16[32,2048]{1,0:T(8,128)(2,1)S(1)}, bf16[32,2048]{1,0:T(8,128)(2,1)S(1)}, bf16[32,2048]{1,0:T(8,128)(2,1)S(1)}, bf16[32,2048]{1,0:T(8,128)(2,1)S(1)}) custom-call(bf16[32,2176]{1,0:T(8,128)(2,1)S(1)} %shard_map.113.refs_0_, bf16[32,2176]{1,0:T(8,128)(2,1)S(1)} %collective-permute-done.1.refs_1_, ...), custom_call_target="tpu_custom_call" | custom-call | tf_op jit(solution)/shard_map/pallas_call | solution.py:16
  24.3 0.9 %collective-permute-start.6 = (bf16[32,2048]{1,0:T(8,128)(2,1)S(1)}, bf16[32,2048]{1,0:T(8,128)(2,1)S(1)}, u32[]{:S(2)}, u32[]{:S(2)}) collective-permute-start(bf16[32,2048]{1,0:T(8,128)(2,1)S(1)} %get-tuple-element.24), channel_id=1, source_target_pairs={{0,2},{1,3},{2,0},{3,1},{4,6},{5,7},{6,4},{7,5},{8,10},{9,11},{10,... | collective-permute-start | bytes 393224 | tf_op jit(solution)/shard_map/ppermute | solution.py:36
  25.3 1.8 %collective-permute-start.7 = (bf16[32,2048]{1,0:T(8,128)(2,1)S(1)}, bf16[32,2048]{1,0:T(8,128)(2,1)S(1)}, u32[]{:S(2)}, u32[]{:S(2)}) collective-permute-start(bf16[32,2048]{1,0:T(8,128)(2,1)S(1)} %get-tuple-element.25), channel_id=1, source_target_pairs={{0,4},{1,5},{2,6},{3,7},{4,0},{5,1},{6,2},{7,3},{8,12},{9,13},{10,... | collective-permute-start | bytes 393224 | tf_op jit(solution)/shard_map/ppermute | solution.py:36
  27.1 0.0 collective-permute-done.12.refs_1_
  27.1 1.3 %collective-permute-start.8 = (bf16[32,2048]{1,0:T(8,128)(2,1)S(1)}, bf16[32,2048]{1,0:T(8,128)(2,1)S(1)}, u32[]{:S(2)}, u32[]{:S(2)}) collective-permute-start(bf16[32,2048]{1,0:T(8,128)(2,1)S(1)} %get-tuple-element.26), channel_id=1, source_target_pairs={{0,6},{1,7},{2,4},{3,5},{4,2},{5,3},{6,0},{7,1},{8,14},{9,15},{10,... | collective-permute-start | bytes 393224 | tf_op jit(solution)/shard_map/ppermute | solution.py:36
  28.4 0.0 collective-permute-done.13.refs_2_
  28.4 0.4 collective-permute-done.14.refs_3_
  28.7 1.6 %shard_map.118 = (bf16[32,2048]{1,0:T(8,128)(2,1)S(1)}, bf16[32,2048]{1,0:T(8,128)(2,1)S(1)}, bf16[32,2048]{1,0:T(8,128)(2,1)S(1)}, bf16[32,2048]{1,0:T(8,128)(2,1)S(1)}) custom-call(bf16[32,2176]{1,0:T(8,128)(2,1)S(1)} %shard_map.117.refs_0_, bf16[32,2176]{1,0:T(8,128)(2,1)S(1)} %collective-permute-done.12.refs_1_, ...), custom_call_target="tpu_custom_call" | custom-call | tf_op jit(solution)/shard_map/pallas_call | solution.py:16
  30.4 1.2 %collective-permute-start.15 = (bf16[32,2048]{1,0:T(8,128)(2,1)S(1)}, bf16[32,2048]{1,0:T(8,128)(2,1)S(1)}, u32[]{:S(2)}, u32[]{:S(2)}) collective-permute-start(bf16[32,2048]{1,0:T(8,128)(2,1)S(1)} %get-tuple-element.31), channel_id=1, source_target_pairs={{0,2},{1,3},{2,0},{3,1},{4,6},{5,7},{6,4},{7,5},{8,10},{9,11},{10,... | collective-permute-start | bytes 393224 | tf_op jit(solution)/shard_map/ppermute | solution.py:36
  31.6 2.5 %collective-permute-start.16 = (bf16[32,2048]{1,0:T(8,128)(2,1)S(1)}, bf16[32,2048]{1,0:T(8,128)(2,1)S(1)}, u32[]{:S(2)}, u32[]{:S(2)}) collective-permute-start(bf16[32,2048]{1,0:T(8,128)(2,1)S(1)} %get-tuple-element.32), channel_id=1, source_target_pairs={{0,4},{1,5},{2,6},{3,7},{4,0},{5,1},{6,2},{7,3},{8,12},{9,13},{10,... | collective-permute-start | bytes 393224 | tf_op jit(solution)/shard_map/ppermute | solution.py:36
  34.1 0.0 collective-permute-done.6.refs_1_
  34.1 0.0 collective-permute-start.17
  34.1 0.8 %collective-permute-done.8.refs_3_ = bf16[32,2048]{1,0:T(8,128)(2,1)S(1)} collective-permute-done((bf16[32,2048]{1,0:T(8,128)(2,1)S(1)}, bf16[32,2048]{1,0:T(8,128)(2,1)S(1)}, u32[]{:S(2)}, u32[]{:S(2)}) %collective-permute-start.8) | collective-permute-done | bytes 131104 | tf_op jit(solution)/shard_map/ppermute | solution.py:36
  34.9 0.1 shard_map.116
  35.0 3.1 %collective-permute-start.9 = (bf16[16,2048]{1,0:T(8,128)(2,1)S(1)}, bf16[16,2048]{1,0:T(8,128)(2,1)S(1)}, u32[]{:S(2)}, u32[]{:S(2)}) collective-permute-start(bf16[16,2048]{1,0:T(8,128)(2,1)S(1)} %get-tuple-element.27), channel_id=1, source_target_pairs={{0,24},{1,25},{2,26},{3,27},{4,28},{5,29},{6,30},{7,31},{8,16},{9,... | collective-permute-start | bytes 196616 | tf_op jit(solution)/shard_map/ppermute | solution.py:36
  38.0 0.0 collective-permute-done.15.refs_1_
  38.0 1.9 %collective-permute-done.17.refs_3_ = bf16[32,2048]{1,0:T(8,128)(2,1)S(1)} collective-permute-done((bf16[32,2048]{1,0:T(8,128)(2,1)S(1)}, bf16[32,2048]{1,0:T(8,128)(2,1)S(1)}, u32[]{:S(2)}, u32[]{:S(2)}) %collective-permute-start.17) | collective-permute-done | bytes 131104 | tf_op jit(solution)/shard_map/ppermute | solution.py:36
  40.0 0.1 shard_map.119
  40.0 0.5 collective-permute-start.18
  40.5 1.9 %collective-permute-start.19 = (bf16[16,2048]{1,0:T(8,128)(2,1)S(1)}, bf16[16,2048]{1,0:T(8,128)(2,1)S(1)}, u32[]{:S(2)}, u32[]{:S(2)}) collective-permute-start(bf16[16,2048]{1,0:T(8,128)(2,1)S(1)} %get-tuple-element.35), channel_id=1, source_target_pairs={{0,8},{1,9},{2,10},{3,11},{4,12},{5,13},{6,14},{7,15},{8,0},{9,1},... | collective-permute-start | bytes 196616 | tf_op jit(solution)/shard_map/ppermute | solution.py:36
  42.4 0.0 collective-permute-done.9.refs_0_
  42.4 3.1 %collective-permute-done.18.refs_2_ = bf16[16,2048]{1,0:T(8,128)(2,1)S(1)} collective-permute-done((bf16[16,2048]{1,0:T(8,128)(2,1)S(1)}, bf16[16,2048]{1,0:T(8,128)(2,1)S(1)}, u32[]{:S(2)}, u32[]{:S(2)}) %collective-permute-start.18) | collective-permute-done | bytes 65568 | tf_op jit(solution)/shard_map/ppermute | solution.py:36
  45.5 0.0 collective-permute-done.19.refs_3_
  45.5 0.7 %shard_map.120 = (bf16[8,2048]{1,0:T(8,128)(2,1)}, bf16[8,2048]{1,0:T(8,128)(2,1)}, f32[32,16]{1,0:T(8,128)S(1)}) custom-call(bf16[16,2048]{1,0:T(8,128)(2,1)S(1)} %collective-permute-done.9.refs_0_, f32[16,2048]{1,0:T(8,128)S(1)} %get-tuple-element.28.refs_1_, bf16[16,2048]{1,0:T(8,128)(2,1)S(1)} %collective-permute-done.18.refs_2_, ...), custom_call_target="tpu_custom_call" | custom-call | tf_op jit(solution)/shard_map/pallas_call | solution.py:16
  46.2 10.3 %all_to_all.11 = f32[32,1,16]{2,1,0:T(1,128)S(1)} all-to-all(f32[32,1,16]{2,1,0:T(1,128)S(1)} %bitcast.19), channel_id=1, replica_groups=mesh['section'=1,'expert'=32] {'expert'}, dimensions={0} | all-to-all | bytes 4096 | tf_op jit(solution)/shard_map/all_to_all | solution.py:331
  56.6 0.5 shard_map.121
  (8 shorter events, 0.0 us)
Async XLA Ops:
  0.6 18.4 %collective-permute-start.4 = (bf16[2048,768]{1,0:T(8,128)(2,1)}, bf16[2048,768]{1,0:T(8,128)(2,1)S(1)}, u32[]{:S(2)}, u32[]{:S(2)}) collective-permute-start(bf16[2048,768]{1,0:T(8,128)(2,1)} %bitcast.20), channel_id=1, source_target_pairs={{0,1},{1,0},{2,3},{3,2},{4,5},{5,4},{6,7},{7,6},{8,9},{9,8},{10,11... | collective-permute-start | bytes 9437192 | tf_op jit(solution)/shard_map/ppermute | solution.py:36
  1.1 17.9 %collective-permute-start.5 = (bf16[384,2048]{1,0:T(8,128)(2,1)}, bf16[384,2048]{1,0:T(8,128)(2,1)S(1)}, u32[]{:S(2)}, u32[]{:S(2)}) collective-permute-start(bf16[384,2048]{1,0:T(8,128)(2,1)} %bitcast.22), channel_id=1, source_target_pairs={{0,1},{1,0},{2,3},{3,2},{4,5},{5,4},{6,7},{7,6},{8,9},{9,8},{10,11... | collective-permute-start | bytes 4718600 | tf_op jit(solution)/shard_map/ppermute | solution.py:36
  3.1 8.1 %collective-permute-start = (bf16[16,2176]{1,0:T(8,128)(2,1)S(1)}, bf16[16,2176]{1,0:T(8,128)(2,1)S(1)}, u32[]{:S(2)}, u32[]{:S(2)}) collective-permute-start(bf16[16,2176]{1,0:T(8,128)(2,1)S(1)} %shard_map.112.refs_0_), channel_id=1, source_target_pairs={{0,24},{1,25},{2,26},{3,27},{4,28},{5,29},{6,30},{7,31},{8,16},{9,... | collective-permute-start | bytes 208904 | tf_op jit(solution)/shard_map/ppermute | solution.py:36
  8.2 5.0 %collective-permute-start.10 = (bf16[16,2176]{1,0:T(8,128)(2,1)S(1)}, bf16[16,2176]{1,0:T(8,128)(2,1)S(1)}, u32[]{:S(2)}, u32[]{:S(2)}) collective-permute-start(bf16[16,2176]{1,0:T(8,128)(2,1)S(1)} %shard_map.112.refs_0_), channel_id=1, source_target_pairs={{0,8},{1,9},{2,10},{3,11},{4,12},{5,13},{6,14},{7,15},{8,0},{9,1},... | collective-permute-start | bytes 208904 | tf_op jit(solution)/shard_map/ppermute | solution.py:36
  8.2 6.7 %collective-permute-start.11 = (bf16[16,2176]{1,0:T(8,128)(2,1)S(1)}, bf16[16,2176]{1,0:T(8,128)(2,1)S(1)}, u32[]{:S(2)}, u32[]{:S(2)}) collective-permute-start(bf16[16,2176]{1,0:T(8,128)(2,1)S(1)} %shard_map.112.refs_0_), channel_id=1, source_target_pairs={{0,16},{1,17},{2,18},{3,19},{4,20},{5,21},{6,22},{7,23},{8,24},{9,... | collective-permute-start | bytes 208904 | tf_op jit(solution)/shard_map/ppermute | solution.py:36
  11.2 9.7 %collective-permute-start.1 = (bf16[32,2176]{1,0:T(8,128)(2,1)S(1)}, bf16[32,2176]{1,0:T(8,128)(2,1)S(1)}, u32[]{:S(2)}, u32[]{:S(2)}) collective-permute-start(bf16[32,2176]{1,0:T(8,128)(2,1)S(1)} %shard_map.113.refs_0_), channel_id=1, source_target_pairs={{0,2},{1,3},{2,0},{3,1},{4,6},{5,7},{6,4},{7,5},{8,10},{9,11},{10,... | collective-permute-start | bytes 417800 | tf_op jit(solution)/shard_map/ppermute | solution.py:36
  13.2 9.4 %collective-permute-start.2 = (bf16[32,2176]{1,0:T(8,128)(2,1)S(1)}, bf16[32,2176]{1,0:T(8,128)(2,1)S(1)}, u32[]{:S(2)}, u32[]{:S(2)}) collective-permute-start(bf16[32,2176]{1,0:T(8,128)(2,1)S(1)} %shard_map.113.refs_0_), channel_id=1, source_target_pairs={{0,4},{1,5},{2,6},{3,7},{4,0},{5,1},{6,2},{7,3},{8,12},{9,13},{10,... | collective-permute-start | bytes 417800 | tf_op jit(solution)/shard_map/ppermute | solution.py:36
  14.9 7.7 %collective-permute-start.3 = (bf16[32,2176]{1,0:T(8,128)(2,1)S(1)}, bf16[32,2176]{1,0:T(8,128)(2,1)S(1)}, u32[]{:S(2)}, u32[]{:S(2)}) collective-permute-start(bf16[32,2176]{1,0:T(8,128)(2,1)S(1)} %shard_map.113.refs_0_), channel_id=1, source_target_pairs={{0,6},{1,7},{2,4},{3,5},{4,2},{5,3},{6,0},{7,1},{8,14},{9,15},{10,... | collective-permute-start | bytes 417800 | tf_op jit(solution)/shard_map/ppermute | solution.py:36
  19.0 8.1 %collective-permute-start.12 = (bf16[32,2176]{1,0:T(8,128)(2,1)S(1)}, bf16[32,2176]{1,0:T(8,128)(2,1)S(1)}, u32[]{:S(2)}, u32[]{:S(2)}) collective-permute-start(bf16[32,2176]{1,0:T(8,128)(2,1)S(1)} %shard_map.117.refs_0_), channel_id=1, source_target_pairs={{0,2},{1,3},{2,0},{3,1},{4,6},{5,7},{6,4},{7,5},{8,10},{9,11},{10,... | collective-permute-start | bytes 417800 | tf_op jit(solution)/shard_map/ppermute | solution.py:36
  19.6 8.7 %collective-permute-start.13 = (bf16[32,2176]{1,0:T(8,128)(2,1)S(1)}, bf16[32,2176]{1,0:T(8,128)(2,1)S(1)}, u32[]{:S(2)}, u32[]{:S(2)}) collective-permute-start(bf16[32,2176]{1,0:T(8,128)(2,1)S(1)} %shard_map.117.refs_0_), channel_id=1, source_target_pairs={{0,4},{1,5},{2,6},{3,7},{4,0},{5,1},{6,2},{7,3},{8,12},{9,13},{10,... | collective-permute-start | bytes 417800 | tf_op jit(solution)/shard_map/ppermute | solution.py:36
  20.9 7.9 %collective-permute-start.14 = (bf16[32,2176]{1,0:T(8,128)(2,1)S(1)}, bf16[32,2176]{1,0:T(8,128)(2,1)S(1)}, u32[]{:S(2)}, u32[]{:S(2)}) collective-permute-start(bf16[32,2176]{1,0:T(8,128)(2,1)S(1)} %shard_map.117.refs_0_), channel_id=1, source_target_pairs={{0,6},{1,7},{2,4},{3,5},{4,2},{5,3},{6,0},{7,1},{8,14},{9,15},{10,... | collective-permute-start | bytes 417800 | tf_op jit(solution)/shard_map/ppermute | solution.py:36
  24.3 9.8 %collective-permute-start.6 = (bf16[32,2048]{1,0:T(8,128)(2,1)S(1)}, bf16[32,2048]{1,0:T(8,128)(2,1)S(1)}, u32[]{:S(2)}, u32[]{:S(2)}) collective-permute-start(bf16[32,2048]{1,0:T(8,128)(2,1)S(1)} %get-tuple-element.24), channel_id=1, source_target_pairs={{0,2},{1,3},{2,0},{3,1},{4,6},{5,7},{6,4},{7,5},{8,10},{9,11},{10,... | collective-permute-start | bytes 393224 | tf_op jit(solution)/shard_map/ppermute | solution.py:36
  25.3 8.8 %collective-permute-start.7 = (bf16[32,2048]{1,0:T(8,128)(2,1)S(1)}, bf16[32,2048]{1,0:T(8,128)(2,1)S(1)}, u32[]{:S(2)}, u32[]{:S(2)}) collective-permute-start(bf16[32,2048]{1,0:T(8,128)(2,1)S(1)} %get-tuple-element.25), channel_id=1, source_target_pairs={{0,4},{1,5},{2,6},{3,7},{4,0},{5,1},{6,2},{7,3},{8,12},{9,13},{10,... | collective-permute-start | bytes 393224 | tf_op jit(solution)/shard_map/ppermute | solution.py:36
  27.1 18.4 %copy-start = (s32[1,1,8,8]{3,2,1,0:T(8,128)S(1)}, s32[1,1,8,8]{3,2,1,0:T(8,128)}, u32[]{:S(2)}) copy-start(s32[1,1,8,8]{3,2,1,0:T(8,128)} %param.11) | copy-start | bytes 772
  27.1 18.4 %copy-start.1 = (f32[1,1,8,8]{3,2,1,0:T(8,128)S(1)}, f32[1,1,8,8]{3,2,1,0:T(8,128)}, u32[]{:S(2)}) copy-start(f32[1,1,8,8]{3,2,1,0:T(8,128)} %param.13) | copy-start | bytes 772
  27.1 7.8 %collective-permute-start.8 = (bf16[32,2048]{1,0:T(8,128)(2,1)S(1)}, bf16[32,2048]{1,0:T(8,128)(2,1)S(1)}, u32[]{:S(2)}, u32[]{:S(2)}) collective-permute-start(bf16[32,2048]{1,0:T(8,128)(2,1)S(1)} %get-tuple-element.26), channel_id=1, source_target_pairs={{0,6},{1,7},{2,4},{3,5},{4,2},{5,3},{6,0},{7,1},{8,14},{9,15},{10,... | collective-permute-start | bytes 393224 | tf_op jit(solution)/shard_map/ppermute | solution.py:36
  30.4 7.6 %collective-permute-start.15 = (bf16[32,2048]{1,0:T(8,128)(2,1)S(1)}, bf16[32,2048]{1,0:T(8,128)(2,1)S(1)}, u32[]{:S(2)}, u32[]{:S(2)}) collective-permute-start(bf16[32,2048]{1,0:T(8,128)(2,1)S(1)} %get-tuple-element.31), channel_id=1, source_target_pairs={{0,2},{1,3},{2,0},{3,1},{4,6},{5,7},{6,4},{7,5},{8,10},{9,11},{10,... | collective-permute-start | bytes 393224 | tf_op jit(solution)/shard_map/ppermute | solution.py:36
  31.6 6.4 %collective-permute-start.16 = (bf16[32,2048]{1,0:T(8,128)(2,1)S(1)}, bf16[32,2048]{1,0:T(8,128)(2,1)S(1)}, u32[]{:S(2)}, u32[]{:S(2)}) collective-permute-start(bf16[32,2048]{1,0:T(8,128)(2,1)S(1)} %get-tuple-element.32), channel_id=1, source_target_pairs={{0,4},{1,5},{2,6},{3,7},{4,0},{5,1},{6,2},{7,3},{8,12},{9,13},{10,... | collective-permute-start | bytes 393224 | tf_op jit(solution)/shard_map/ppermute | solution.py:36
  34.1 5.9 %collective-permute-start.17 = (bf16[32,2048]{1,0:T(8,128)(2,1)S(1)}, bf16[32,2048]{1,0:T(8,128)(2,1)S(1)}, u32[]{:S(2)}, u32[]{:S(2)}) collective-permute-start(bf16[32,2048]{1,0:T(8,128)(2,1)S(1)} %get-tuple-element.33), channel_id=1, source_target_pairs={{0,6},{1,7},{2,4},{3,5},{4,2},{5,3},{6,0},{7,1},{8,14},{9,15},{10,... | collective-permute-start | bytes 393224 | tf_op jit(solution)/shard_map/ppermute | solution.py:36
  35.0 7.5 %collective-permute-start.9 = (bf16[16,2048]{1,0:T(8,128)(2,1)S(1)}, bf16[16,2048]{1,0:T(8,128)(2,1)S(1)}, u32[]{:S(2)}, u32[]{:S(2)}) collective-permute-start(bf16[16,2048]{1,0:T(8,128)(2,1)S(1)} %get-tuple-element.27), channel_id=1, source_target_pairs={{0,24},{1,25},{2,26},{3,27},{4,28},{5,29},{6,30},{7,31},{8,16},{9,... | collective-permute-start | bytes 196616 | tf_op jit(solution)/shard_map/ppermute | solution.py:36
  40.0 5.5 %collective-permute-start.18 = (bf16[16,2048]{1,0:T(8,128)(2,1)S(1)}, bf16[16,2048]{1,0:T(8,128)(2,1)S(1)}, u32[]{:S(2)}, u32[]{:S(2)}) collective-permute-start(bf16[16,2048]{1,0:T(8,128)(2,1)S(1)} %get-tuple-element.34), channel_id=1, source_target_pairs={{0,16},{1,17},{2,18},{3,19},{4,20},{5,21},{6,22},{7,23},{8,24},{9,... | collective-permute-start | bytes 196616 | tf_op jit(solution)/shard_map/ppermute | solution.py:36
  40.5 5.0 %collective-permute-start.19 = (bf16[16,2048]{1,0:T(8,128)(2,1)S(1)}, bf16[16,2048]{1,0:T(8,128)(2,1)S(1)}, u32[]{:S(2)}, u32[]{:S(2)}) collective-permute-start(bf16[16,2048]{1,0:T(8,128)(2,1)S(1)} %get-tuple-element.35), channel_id=1, source_target_pairs={{0,8},{1,9},{2,10},{3,11},{4,12},{5,13},{6,14},{7,15},{8,0},{9,1},... | collective-permute-start | bytes 196616 | tf_op jit(solution)/shard_map/ppermute | solution.py:36
